TPU v7x, 128 devices: a whole 4x4x4 slice. The times are simulated.
128 devices in a mesh: group: 4 (over y), batch: 32 (over z, x, core).
Axes of the slice: x: 4, y: 4, z: 4, core: 2. Of those that a mesh axis runs over, the one named last changes fastest.
Arguments:
- queries: bfloat16 [49152, 256], P(('group', 'batch')), may hold values from -20 to 20
- pos_emb: bfloat16 [49152, 256], P(('group', 'batch')), may hold values from -6 to 6
- pos_logq: bfloat16 [49152], P(('group', 'batch')), may hold values from -14 to -11
- pos_ids: int32 [49152], P(('group', 'batch')), may hold values from 0 to 8388607
- row_weight: float32 [49152], P(('group', 'batch')), may hold values from 1 to 16
- neg_emb: bfloat16 [16384, 256], P(('group', 'batch')), may hold values from -5 to 5
- neg_logq: bfloat16 [16384], P(('group', 'batch')), may hold values from -14 to -11
- neg_ids: int32 [16384], P(('group', 'batch')), may hold values from 0 to 8388607
- neg_owner: int32 [16384], P(('group', 'batch')), may hold values from 0 to 3, as said below
- neg_slot: int32 [16384], P(('group', 'batch')), may hold values from 0 to 511
Outputs:
- query_grad: float32 [49152, 256], P(('group', 'batch'))
- item_grad: float32 [49152, 256], P(('group', 'batch'))
- table_grad: float32 [65536, 256], P(('group', 'batch'))
Inputs may be any that keep to these rules, and one draw needn't show every extreme that they name: `neg_owner`: each device sends exactly 64 of its sampled rows to one owner group, the same group for all devices with the same batch index, and its other rows to the other groups.
All inputs are finite; a program needn't handle non-finite values.
Results may differ from a plain program's by a relative error of at most 0.0035.
Values may be sent and summed in bfloat16 or wider, within the bound.
A program may use at most 128 MiB of HBM per device.

v0:
```python
import math

import jax
import jax.numpy as jnp
from jax import lax
from jax.sharding import PartitionSpec as P

SLOTS = 512


score_scale = 0.125
masked_floor = -1e30


def local(
    queries, pos_emb, pos_logq, pos_ids, row_weight, neg_emb, neg_logq, neg_ids, neg_owner, neg_slot
):
    row_count = queries.shape[0]
    neg_count = neg_emb.shape[0]
    features = queries.shape[1]
    per_device = row_count + neg_count
    shard_count = lax.axis_size("batch")
    group_count = lax.axis_size("group")
    my_index = lax.axis_index("batch")
    local_cands = jnp.concatenate([pos_emb, neg_emb], axis=0)
    local_logq = jnp.concatenate([pos_logq, neg_logq], axis=0)
    local_ids = jnp.concatenate([pos_ids, neg_ids], axis=0)
    candidates, cand_logq, cand_ids = (
        lax.all_gather(local_cands, "batch", axis=0, tiled=True),
        lax.all_gather(local_logq, "batch", axis=0, tiled=True),
        lax.all_gather(local_ids, "batch", axis=0, tiled=True),
    )
    shards_per_block = math.gcd(shard_count, max(1, 2048 // per_device))
    block_cols = shards_per_block * per_device
    block_count = shard_count // shards_per_block
    targets = my_index * per_device + jnp.arange(row_count, dtype=jnp.int32)

    def block_scores(offset):
        block_cands = lax.dynamic_slice_in_dim(candidates, offset, block_cols, 0)
        block_logq = lax.dynamic_slice_in_dim(cand_logq, offset, block_cols, 0).astype(jnp.float32)
        block_ids = lax.dynamic_slice_in_dim(cand_ids, offset, block_cols, 0)
        products = lax.dot_general(
            block_cands, queries, (((1,), (1,)), ((), ())), preferred_element_type=jnp.float32
        )
        scores = products * score_scale - block_logq[:, None]
        cand_index = offset + jnp.arange(block_cols, dtype=jnp.int32)
        is_target = cand_index[:, None] == targets[None, :]
        allowed = jnp.logical_or(block_ids[:, None] != pos_ids[None, :], is_target)
        return (block_cands, scores, allowed, is_target)

    def stats_step(block_index, stats_state):
        row_max, row_sum = stats_state
        block_cands, scores, allowed, is_target = block_scores(block_index * block_cols)
        new_max = jnp.maximum(row_max, jnp.max(jnp.where(allowed, scores, masked_floor), axis=0))
        kept_terms = jnp.where(allowed, jnp.exp(scores - new_max[None, :]), 0.0)
        return (new_max, row_sum * jnp.exp(row_max - new_max) + jnp.sum(kept_terms, axis=0))

    start_state = (
        jnp.full((row_count,), masked_floor, jnp.float32),
        jnp.zeros((row_count,), jnp.float32),
    )
    row_max, row_sum = lax.fori_loop(0, block_count, stats_step, start_state)
    row_lse = row_max + jnp.log(row_sum)

    def grad_block(offset):
        block_cands, scores, allowed, is_target = block_scores(offset)
        soft_weights = jnp.where(allowed, jnp.exp(scores - row_lse[None, :]), 0.0)
        grad_rows = (row_weight[None, :] * (soft_weights - is_target.astype(jnp.float32))).astype(
            jnp.bfloat16
        )
        return (block_cands, grad_rows)

    def make_block(block_index):
        block_cands, grad_rows = grad_block(block_index * block_cols)
        return grad_rows

    grad_cols = lax.map(make_block, jnp.arange(block_count, dtype=jnp.int32)).reshape(
        shard_count * per_device, row_count
    )
    query_grad = (
        lax.dot_general(
            grad_cols, candidates, (((0,), (0,)), ((), ())), preferred_element_type=jnp.float32
        )
        * score_scale
    )
    own_grads = lax.psum_scatter(
        jnp.dot(grad_cols, queries, preferred_element_type=jnp.float32) * score_scale,
        "batch",
        scatter_dimension=0,
        tiled=True,
    )
    item_grad = own_grads[:row_count]
    sampled_grad = own_grads[row_count:]
    capacity = neg_count // 2
    owner_match = (neg_owner[:, None] == jnp.arange(group_count, dtype=jnp.int32)[None, :]).astype(
        jnp.int32
    )
    earlier = jnp.cumsum(owner_match, axis=0) - owner_match
    order_in = jnp.sum(earlier * owner_match, axis=1)
    destination = neg_owner * capacity + order_in
    send_rows = (
        jnp.zeros((group_count * capacity, features), jnp.float32)
        .at[destination]
        .set(sampled_grad)
        .reshape(group_count, capacity, features)
    )
    send_slots = (
        jnp.zeros((group_count * capacity,), jnp.int32)
        .at[destination]
        .set(neg_slot)
        .reshape(group_count, capacity)
    )
    got_rows, got_slots = (
        lax.all_to_all(send_rows, "group", split_axis=0, concat_axis=0, tiled=True),
        lax.all_to_all(send_slots, "group", split_axis=0, concat_axis=0, tiled=True),
    )
    table_grad = (
        jnp.zeros((SLOTS, features), jnp.float32)
        .at[got_slots.reshape(-1)]
        .add(got_rows.reshape(-1, features))
    )
    return (query_grad, item_grad, table_grad)


def solution(mesh):
    in_specs = (
        P(("group", "batch"), None),
        P(("group", "batch"), None),
        P(("group", "batch")),
        P(("group", "batch")),
        P(("group", "batch")),
        P(("group", "batch"), None),
        P(("group", "batch")),
        P(("group", "batch")),
        P(("group", "batch")),
        P(("group", "batch")),
    )
    out_specs = (
        P(("group", "batch"), None),
        P(("group", "batch"), None),
        P(("group", "batch"), None),
    )
    return jax.shard_map(local, mesh=mesh, in_specs=in_specs, out_specs=out_specs, check_vma=False)
```

profile of v0, /device:TPU:1, one launch (start us, length us, event | category | flops | bytes accessed | tf_op | source)
XLA Modules:
  0.0 300.2 jit_solution(13515532034697469676)
XLA Ops:
  7.2 1.7 pad_maximum_fusion
  9.7 26.8 %all-gather.1 = bf16[32,1,512]{2,1,0:T(2,128)(2,1)S(1)} all-gather(bf16[1,1,512]{2,1,0:T(2,128)(2,1)S(1)} %reshape.105), channel_id=1, replica_groups=mesh['group'=4,'batch'=32] {'batch'}, dimensions={0}, use_global_device_ids=true | all-gather | bytes 33792 | tf_op jit(solution)/shard_map/all_gather | solution.py:30
  37.5 23.5 %all-gather = s32[32,1,512]{2,1,0:T(1,128)S(1)} all-gather(s32[1,1,512]{2,1,0:T(1,128)S(1)} %bitcast.33), channel_id=1, replica_groups=mesh['group'=4,'batch'=32] {'batch'}, dimensions={0}, use_global_device_ids=true | all-gather | bytes 67584 | tf_op jit(solution)/shard_map/all_gather | solution.py:31
  61.0 6.7 %all-gather.4.cloned.1.call-done = bf16[16384,256]{1,0:T(8,128)(2,1)} async-done(((bf16[512,256]{1,0:T(8,128)(2,1)}), bf16[16384,256]{1,0:T(8,128)(2,1)}) %all-gather.4.cloned.1.call-update) | async-done | bytes 8388624 | tf_op jit(solution)/shard_map/all_gather | solution.py:29
  67.7 37.3 %while.28 = (s32[]{:T(128)}, f32[384]{0:T(512)S(1)}, f32[384]{0:T(512)S(1)}, s32[16384]{0:T(1024)S(1)}, s32[384]{0:T(512)}, /*index=5*/bf16[16384,256]{1,0:T(8,1...) while((s32[]{:T(128)}, f32[384]{0:T(512)S(1)}, ...), condition=%wide.region_3.4_spmd.clone, body=%wide.region_0.3_spmd.clone.sunk | while | flops 412883200 | bytes 7649006 | solution.py:62
  67.8 3.2 %select_reduce_fusion.5 = (f32[384]{0:T(512)S(1)}, f32[2048,384]{1,0:T(8,128)S(1)}) fusion(s32[384]{0:T(512)S(1)} %iota_add_fusion.10, s32[384]{0:T(512)} %get-tuple-element.474, s32[2048]{0:T(1024)S(1)} %iota_add_fusion.11, s32[2048]{0:T(1024)S(1)} %dynamic_slice.62, f32[2048]{0:T(1024)S(1)} %dynamic-slice_convert_fusion.5, ...), kind=kOutput, calls=%fused_computation.18.clone.1 | convolution fusion | flops 408157824 | bytes 4420612 | tf_op jit(solution)/shard_map/while/body/eval_jaxpr/dot_general | solution.py:42
  71.0 1.3 select_reduce_fusion.6
  72.4 3.2 %select_reduce_fusion.5 = (f32[384]{0:T(512)S(1)}, f32[2048,384]{1,0:T(8,128)S(1)}) fusion(s32[384]{0:T(512)S(1)} %iota_add_fusion.10, s32[384]{0:T(512)} %get-tuple-element.474, s32[2048]{0:T(1024)S(1)} %iota_add_fusion.11, s32[2048]{0:T(1024)S(1)} %dynamic_slice.62, f32[2048]{0:T(1024)S(1)} %dynamic-slice_convert_fusion.5, ...), kind=kOutput, calls=%fused_computation.18.clone.1 | convolution fusion | flops 408157824 | bytes 4420612 | tf_op jit(solution)/shard_map/while/body/eval_jaxpr/dot_general | solution.py:42
  75.7 1.3 select_reduce_fusion.6
  77.1 3.2 %select_reduce_fusion.5 = (f32[384]{0:T(512)S(1)}, f32[2048,384]{1,0:T(8,128)S(1)}) fusion(s32[384]{0:T(512)S(1)} %iota_add_fusion.10, s32[384]{0:T(512)} %get-tuple-element.474, s32[2048]{0:T(1024)S(1)} %iota_add_fusion.11, s32[2048]{0:T(1024)S(1)} %dynamic_slice.62, f32[2048]{0:T(1024)S(1)} %dynamic-slice_convert_fusion.5, ...), kind=kOutput, calls=%fused_computation.18.clone.1 | convolution fusion | flops 408157824 | bytes 4420612 | tf_op jit(solution)/shard_map/while/body/eval_jaxpr/dot_general | solution.py:42
  80.4 1.3 select_reduce_fusion.6
  81.8 3.2 %select_reduce_fusion.5 = (f32[384]{0:T(512)S(1)}, f32[2048,384]{1,0:T(8,128)S(1)}) fusion(s32[384]{0:T(512)S(1)} %iota_add_fusion.10, s32[384]{0:T(512)} %get-tuple-element.474, s32[2048]{0:T(1024)S(1)} %iota_add_fusion.11, s32[2048]{0:T(1024)S(1)} %dynamic_slice.62, f32[2048]{0:T(1024)S(1)} %dynamic-slice_convert_fusion.5, ...), kind=kOutput, calls=%fused_computation.18.clone.1 | convolution fusion | flops 408157824 | bytes 4420612 | tf_op jit(solution)/shard_map/while/body/eval_jaxpr/dot_general | solution.py:42
  86.4 3.2 %select_reduce_fusion.5 = (f32[384]{0:T(512)S(1)}, f32[2048,384]{1,0:T(8,128)S(1)}) fusion(s32[384]{0:T(512)S(1)} %iota_add_fusion.10, s32[384]{0:T(512)} %get-tuple-element.474, s32[2048]{0:T(1024)S(1)} %iota_add_fusion.11, s32[2048]{0:T(1024)S(1)} %dynamic_slice.62, f32[2048]{0:T(1024)S(1)} %dynamic-slice_convert_fusion.5, ...), kind=kOutput, calls=%fused_computation.18.clone.1 | convolution fusion | flops 408157824 | bytes 4420612 | tf_op jit(solution)/shard_map/while/body/eval_jaxpr/dot_general | solution.py:42
  91.1 3.2 %select_reduce_fusion.5 = (f32[384]{0:T(512)S(1)}, f32[2048,384]{1,0:T(8,128)S(1)}) fusion(s32[384]{0:T(512)S(1)} %iota_add_fusion.10, s32[384]{0:T(512)} %get-tuple-element.474, s32[2048]{0:T(1024)S(1)} %iota_add_fusion.11, s32[2048]{0:T(1024)S(1)} %dynamic_slice.62, f32[2048]{0:T(1024)S(1)} %dynamic-slice_convert_fusion.5, ...), kind=kOutput, calls=%fused_computation.18.clone.1 | convolution fusion | flops 408157824 | bytes 4420612 | tf_op jit(solution)/shard_map/while/body/eval_jaxpr/dot_general | solution.py:42
  95.8 3.2 %select_reduce_fusion.5 = (f32[384]{0:T(512)S(1)}, f32[2048,384]{1,0:T(8,128)S(1)}) fusion(s32[384]{0:T(512)S(1)} %iota_add_fusion.10, s32[384]{0:T(512)} %get-tuple-element.474, s32[2048]{0:T(1024)S(1)} %iota_add_fusion.11, s32[2048]{0:T(1024)S(1)} %dynamic_slice.62, f32[2048]{0:T(1024)S(1)} %dynamic-slice_convert_fusion.5, ...), kind=kOutput, calls=%fused_computation.18.clone.1 | convolution fusion | flops 408157824 | bytes 4420612 | tf_op jit(solution)/shard_map/while/body/eval_jaxpr/dot_general | solution.py:42
  100.4 3.2 %select_reduce_fusion.5 = (f32[384]{0:T(512)S(1)}, f32[2048,384]{1,0:T(8,128)S(1)}) fusion(s32[384]{0:T(512)S(1)} %iota_add_fusion.10, s32[384]{0:T(512)} %get-tuple-element.474, s32[2048]{0:T(1024)S(1)} %iota_add_fusion.11, s32[2048]{0:T(1024)S(1)} %dynamic_slice.62, f32[2048]{0:T(1024)S(1)} %dynamic-slice_convert_fusion.5, ...), kind=kOutput, calls=%fused_computation.18.clone.1 | convolution fusion | flops 408157824 | bytes 4420612 | tf_op jit(solution)/shard_map/while/body/eval_jaxpr/dot_general | solution.py:42
  105.0 39.2 %while.27 = (s32[]{:T(128)}, bf16[8,2048,384]{2,1,0:T(8,128)(2,1)}, f32[384]{0:T(512)S(1)}, s32[8]{0:T(128)S(1)}, s32[16384]{0:T(1024)S(1)}, /*index=5*/s32[384]...) while((s32[]{:T(128)}, bf16[8,2048,384]{2,1,0:T(8,128)(2,1)}, ...), condition=%wide.region_5.6_spmd.clone, body=%wide.region_4.5_spmd.clone.sunk | while | flops 411308416 | bytes 2887911 | solution.py:77
  106.4 3.6 %fusion.35 = bf16[8,2048,384]{2,1,0:T(8,128)(2,1)} fusion(bf16[8,2048,384]{2,1,0:T(8,128)(2,1)} %get-tuple-element.499, s32[]{:T(128)S(6)} %copy.26, bf16[384,256]{1,0:T(8,128)(2,1)} %get-tuple-element.520, f32[384]{0:T(512)S(1)} %get-tuple-element.522, f32[2048]{0:T(1024)S(1)} %dynamic-slice_convert_fusion.4, s32[384]{0:T(512)S(1)} %iota_add_fusion.8, ...), kind=kOutput, calls=%fused_computation.11.clone.1 | convolution fusion | flops 411303936 | bytes 2849288 | tf_op jit(solution)/shard_map/while/body/eval_jaxpr/dot_general | solution.py:42
  111.3 3.6 %fusion.35 = bf16[8,2048,384]{2,1,0:T(8,128)(2,1)} fusion(bf16[8,2048,384]{2,1,0:T(8,128)(2,1)} %get-tuple-element.499, s32[]{:T(128)S(6)} %copy.26, bf16[384,256]{1,0:T(8,128)(2,1)} %get-tuple-element.520, f32[384]{0:T(512)S(1)} %get-tuple-element.522, f32[2048]{0:T(1024)S(1)} %dynamic-slice_convert_fusion.4, s32[384]{0:T(512)S(1)} %iota_add_fusion.8, ...), kind=kOutput, calls=%fused_computation.11.clone.1 | convolution fusion | flops 411303936 | bytes 2849288 | tf_op jit(solution)/shard_map/while/body/eval_jaxpr/dot_general | solution.py:42
  116.1 3.6 %fusion.35 = bf16[8,2048,384]{2,1,0:T(8,128)(2,1)} fusion(bf16[8,2048,384]{2,1,0:T(8,128)(2,1)} %get-tuple-element.499, s32[]{:T(128)S(6)} %copy.26, bf16[384,256]{1,0:T(8,128)(2,1)} %get-tuple-element.520, f32[384]{0:T(512)S(1)} %get-tuple-element.522, f32[2048]{0:T(1024)S(1)} %dynamic-slice_convert_fusion.4, s32[384]{0:T(512)S(1)} %iota_add_fusion.8, ...), kind=kOutput, calls=%fused_computation.11.clone.1 | convolution fusion | flops 411303936 | bytes 2849288 | tf_op jit(solution)/shard_map/while/body/eval_jaxpr/dot_general | solution.py:42
  121.0 3.6 %fusion.35 = bf16[8,2048,384]{2,1,0:T(8,128)(2,1)} fusion(bf16[8,2048,384]{2,1,0:T(8,128)(2,1)} %get-tuple-element.499, s32[]{:T(128)S(6)} %copy.26, bf16[384,256]{1,0:T(8,128)(2,1)} %get-tuple-element.520, f32[384]{0:T(512)S(1)} %get-tuple-element.522, f32[2048]{0:T(1024)S(1)} %dynamic-slice_convert_fusion.4, s32[384]{0:T(512)S(1)} %iota_add_fusion.8, ...), kind=kOutput, calls=%fused_computation.11.clone.1 | convolution fusion | flops 411303936 | bytes 2849288 | tf_op jit(solution)/shard_map/while/body/eval_jaxpr/dot_general | solution.py:42
  125.9 3.6 %fusion.35 = bf16[8,2048,384]{2,1,0:T(8,128)(2,1)} fusion(bf16[8,2048,384]{2,1,0:T(8,128)(2,1)} %get-tuple-element.499, s32[]{:T(128)S(6)} %copy.26, bf16[384,256]{1,0:T(8,128)(2,1)} %get-tuple-element.520, f32[384]{0:T(512)S(1)} %get-tuple-element.522, f32[2048]{0:T(1024)S(1)} %dynamic-slice_convert_fusion.4, s32[384]{0:T(512)S(1)} %iota_add_fusion.8, ...), kind=kOutput, calls=%fused_computation.11.clone.1 | convolution fusion | flops 411303936 | bytes 2849288 | tf_op jit(solution)/shard_map/while/body/eval_jaxpr/dot_general | solution.py:42
  130.8 3.7 %fusion.35 = bf16[8,2048,384]{2,1,0:T(8,128)(2,1)} fusion(bf16[8,2048,384]{2,1,0:T(8,128)(2,1)} %get-tuple-element.499, s32[]{:T(128)S(6)} %copy.26, bf16[384,256]{1,0:T(8,128)(2,1)} %get-tuple-element.520, f32[384]{0:T(512)S(1)} %get-tuple-element.522, f32[2048]{0:T(1024)S(1)} %dynamic-slice_convert_fusion.4, s32[384]{0:T(512)S(1)} %iota_add_fusion.8, ...), kind=kOutput, calls=%fused_computation.11.clone.1 | convolution fusion | flops 411303936 | bytes 2849288 | tf_op jit(solution)/shard_map/while/body/eval_jaxpr/dot_general | solution.py:42
  135.8 3.6 %fusion.35 = bf16[8,2048,384]{2,1,0:T(8,128)(2,1)} fusion(bf16[8,2048,384]{2,1,0:T(8,128)(2,1)} %get-tuple-element.499, s32[]{:T(128)S(6)} %copy.26, bf16[384,256]{1,0:T(8,128)(2,1)} %get-tuple-element.520, f32[384]{0:T(512)S(1)} %get-tuple-element.522, f32[2048]{0:T(1024)S(1)} %dynamic-slice_convert_fusion.4, s32[384]{0:T(512)S(1)} %iota_add_fusion.8, ...), kind=kOutput, calls=%fused_computation.11.clone.1 | convolution fusion | flops 411303936 | bytes 2849288 | tf_op jit(solution)/shard_map/while/body/eval_jaxpr/dot_general | solution.py:42
  140.7 3.6 %fusion.35 = bf16[8,2048,384]{2,1,0:T(8,128)(2,1)} fusion(bf16[8,2048,384]{2,1,0:T(8,128)(2,1)} %get-tuple-element.499, s32[]{:T(128)S(6)} %copy.26, bf16[384,256]{1,0:T(8,128)(2,1)} %get-tuple-element.520, f32[384]{0:T(512)S(1)} %get-tuple-element.522, f32[2048]{0:T(1024)S(1)} %dynamic-slice_convert_fusion.4, s32[384]{0:T(512)S(1)} %iota_add_fusion.8, ...), kind=kOutput, calls=%fused_computation.11.clone.1 | convolution fusion | flops 411303936 | bytes 2849288 | tf_op jit(solution)/shard_map/while/body/eval_jaxpr/dot_general | solution.py:42
  144.3 14.8 %convolution_multiply_fusion = f32[16384,256]{1,0:T(8,128)} fusion(bf16[16384,384]{1,0:T(8,128)(2,1)} %bitcast.27, bf16[384,256]{1,0:T(8,128)(2,1)} %get-tuple-element.541), kind=kOutput, calls=%fused_computation.29 | convolution fusion | flops 3225419776 | bytes 29556736 | tf_op jit(solution)/shard_map/dot_general | solution.py:87
  161.4 7.9 %all_to_all.14 = s32[4,1,64]{2,1,0:T(1,128)S(1)} all-to-all(s32[4,1,64]{2,1,0:T(1,128)S(1)} %all_to_all.9), channel_id=1, replica_groups=mesh['group'=4,'batch'=32] {'group'}, dimensions={0} | all-to-all | bytes 2048 | tf_op jit(solution)/shard_map/all_to_all | solution.py:115
  170.6 101.8 %reduce-scatter.2.cloned.1.call-done = f32[512,256]{1,0:T(8,128)} async-done(((f32[16384,256]{1,0:T(8,128)}), f32[512,256]{1,0:T(8,128)}) %reduce-scatter.2.cloned.1.call-update) | async-done | bytes 524304 | tf_op jit(solution)/shard_map/reduce_scatter | solution.py:86
  272.4 2.1 scatter_custom_fusion.1
  274.5 4.0 %all-to-all-start.1 = ((f32[4,64,256]{2,1,0:T(8,128)}), f32[4,64,256]{2,1,0:T(8,128)S(1)}, u32[]{:S(2)}, u32[]{:S(2)}) async-start(f32[4,64,256]{2,1,0:T(8,128)} %bitcast.4), calls=%async_computation.2 | async-start | bytes 524288 | tf_op jit(solution)/shard_map/all_to_all | solution.py:114
  278.5 11.2 %convolution_multiply_fusion.1 = f32[384,256]{1,0:T(8,128)} fusion(bf16[16384,384]{1,0:T(8,128)(2,1)} %bitcast.28, bf16[16384,256]{1,0:T(8,128)(2,1)} %get-tuple-element.534), kind=kOutput, calls=%fused_computation.30 | convolution fusion | flops 3221323776 | bytes 21364736 | tf_op jit(solution)/shard_map/dot_general | solution.py:81
  290.4 2.9 scatter_custom_fusion.2
  (149 shorter events, 17.8 us)
Async XLA Ops:
  7.2 60.5 %all-gather.4.cloned.1.call-start = ((), (), s32[]{:S(2)}) async-start(), calls=%async_computation.3 | async-start | bytes 8650752 | tf_op jit(solution)/shard_map/all_gather | solution.py:29
  8.9 263.5 %reduce-scatter.2.cloned.1.call-start = ((), (), s32[]{:S(2)}) async-start(), calls=%async_computation.4 | async-start | bytes 17301504 | tf_op jit(solution)/shard_map/reduce_scatter | solution.py:86
  67.7 37.3 %copy-start.3 = (f32[384]{0:T(512)S(1)}, f32[384]{0:T(512)}, u32[]{:S(2)}) copy-start(f32[384]{0:T(512)} %param.18) | copy-start | bytes 4612
  67.8 3.3 %copy-start.1 = (s32[384]{0:T(512)S(1)}, s32[384]{0:T(512)}, u32[]{:S(2)}) copy-start(s32[384]{0:T(512)} %get-tuple-element.474) | copy-start | bytes 4612 | tf_op jit(solution)/shard_map/while
  72.4 3.3 %copy-start.1 = (s32[384]{0:T(512)S(1)}, s32[384]{0:T(512)}, u32[]{:S(2)}) copy-start(s32[384]{0:T(512)} %get-tuple-element.474) | copy-start | bytes 4612 | tf_op jit(solution)/shard_map/while
  77.1 3.3 %copy-start.1 = (s32[384]{0:T(512)S(1)}, s32[384]{0:T(512)}, u32[]{:S(2)}) copy-start(s32[384]{0:T(512)} %get-tuple-element.474) | copy-start | bytes 4612 | tf_op jit(solution)/shard_map/while
  81.8 3.3 %copy-start.1 = (s32[384]{0:T(512)S(1)}, s32[384]{0:T(512)}, u32[]{:S(2)}) copy-start(s32[384]{0:T(512)} %get-tuple-element.474) | copy-start | bytes 4612 | tf_op jit(solution)/shard_map/while
  86.4 3.3 %copy-start.1 = (s32[384]{0:T(512)S(1)}, s32[384]{0:T(512)}, u32[]{:S(2)}) copy-start(s32[384]{0:T(512)} %get-tuple-element.474) | copy-start | bytes 4612 | tf_op jit(solution)/shard_map/while
  91.1 3.3 %copy-start.1 = (s32[384]{0:T(512)S(1)}, s32[384]{0:T(512)}, u32[]{:S(2)}) copy-start(s32[384]{0:T(512)} %get-tuple-element.474) | copy-start | bytes 4612 | tf_op jit(solution)/shard_map/while
  95.8 3.3 %copy-start.1 = (s32[384]{0:T(512)S(1)}, s32[384]{0:T(512)}, u32[]{:S(2)}) copy-start(s32[384]{0:T(512)} %get-tuple-element.474) | copy-start | bytes 4612 | tf_op jit(solution)/shard_map/while
  100.4 3.3 %copy-start.1 = (s32[384]{0:T(512)S(1)}, s32[384]{0:T(512)}, u32[]{:S(2)}) copy-start(s32[384]{0:T(512)} %get-tuple-element.474) | copy-start | bytes 4612 | tf_op jit(solution)/shard_map/while
  159.1 0.7 copy-start.2
  274.5 16.0 %all-to-all-start.1 = ((f32[4,64,256]{2,1,0:T(8,128)}), f32[4,64,256]{2,1,0:T(8,128)S(1)}, u32[]{:S(2)}, u32[]{:S(2)}) async-start(f32[4,64,256]{2,1,0:T(8,128)} %bitcast.4), calls=%async_computation.2 | async-start | bytes 524288 | tf_op jit(solution)/shard_map/all_to_all | solution.py:114
  278.5 11.2 %copy-start = (f32[512,256]{1,0:T(8,128)S(1)}, f32[512,256]{1,0:T(8,128)}, u32[]{:S(2)}) copy-start(f32[512,256]{1,0:T(8,128)} %reduce-scatter.2.cloned.1.call-done) | copy-start | bytes 1572868
Sparse Core Ops, SparseCore 0:
  10.8 56.8 all-gather.3
  159.2 113.1 reduce-scatter.1
where the time goes:
time: 302 us; the launch traced here: 300 us
  waiting for transfers between devices  109 us (36%)
  matrix products  80.6 us (27%)
  blocking collectives  58.3 us (19%)
  other arithmetic  18 us (6%)
  between operations  14.1 us (5%)
  local copies, waits for them, and re-layouts  10.2 us (3%)
  loops' own time  6.32 us (2%)
  starting transfers between devices  4.09 us (1%)
    reduce_scatter x1, waiting for transfers between devices, local(): lax.psum_scatter(jnp.dot(grad_cols, queries, preferred_element_type=jnp.f...  102 us
    dot_general x16, matrix products, block_scores(): lax.dot_general(block_cands, queries, (((1,), (1,)), ((), ())), preferred...  54.6 us
    all_gather x1, blocking collectives, local(): lax.all_gather(local_logq, 'batch', axis=0, tiled=True)  26.8 us
    all_gather x1, blocking collectives, local(): lax.all_gather(local_ids, 'batch', axis=0, tiled=True)  23.5 us
    dot_general x1, matrix products, local(): jnp.dot(grad_cols, queries, preferred_element_type=jnp.float32)  14.8 us
    dot_general x1, matrix products, local(): lax.dot_general(grad_cols, candidates, (((0,), (0,)), ((), ())), preferre...  11.2 us
    reduce_sum x8, other arithmetic, stats_step(): jnp.sum(kept_terms, axis=0)  10.2 us
    all_to_all x1, blocking collectives, local(): lax.all_to_all(send_slots, 'group', split_axis=0, concat_axis=0, tiled=True)  7.9 us
  transfers between devices with their start and end apart: 3, of which 2 were waited for; matrix products, arithmetic and copies ran while one was open for 5% of the time, Pallas kernels for 0%

commit v1 on v0

v1 whole, which is shorter than its diff:
```python
import functools
import math

import jax
import jax.numpy as jnp
from jax import lax
from jax.experimental import pallas as pl
from jax.experimental.pallas import tpu as pltpu
from jax.sharding import PartitionSpec as P

MESH = pl.DeviceIdType.MESH
F32 = jnp.float32
BF16 = jnp.bfloat16
LOG2E = math.log2(math.e)
SCALE = 0.125
FLOOR = -1e30

ROWS = 384
NEGS = 128
CANDS = ROWS + NEGS
PAIR = 2 * ROWS
DIM = 256
SLOTS = 512
CHUNK = 32

DIST = (0, 1, 3, 2)
PLACE = (0, 1, 3, 2)


def tiled(x, count):
    return jnp.concatenate([x] * count, axis=1)


def kernel(
    q_in, pos_in, neg_in, cmeta_in, qmeta_in, ymeta_in,
    qgt_out, item_out, table_out,
    cands, cands_t, quers, scores, weights,
    cmeta, qmeta, ymeta, logq_col, id_col, stat, stats, shift,
    cand_part, cand_send, cand_relay, cand_got,
    quer_part, sib_send, sib_got, quer_send, quer_relay, quer_got,
    neg_rows, onehot, local_sem, send_sem, recv_sem,
):
    g = lax.axis_index("group")
    b = lax.axis_index("batch")
    z, x, c = b // 8, (b // 2) % 4, b % 2
    my_abs = x * 2 + c

    def along_z(step):
        return {"batch": ((z + step) % 4) * 8 + x * 2 + c}

    def along_x(step, flip=0):
        core = (1 - c) if flip else c
        return {"batch": z * 8 + ((x + step) % 4) * 2 + core}

    def along_y(step):
        return {"group": (g + step) % 4}

    sems = iter(range(64))
    sent = []

    def remote(src, dst, target, k=None):
        k = next(sems) if k is None else k
        return pltpu.make_async_remote_copy(
            src_ref=src, dst_ref=dst, send_sem=send_sem.at[k], recv_sem=recv_sem.at[k],
            device_id=target, device_id_type=MESH,
        )

    def go(copy):
        copy.start()
        sent.append(copy)

    locals_ = [
        pltpu.make_async_copy(q_in, quers.at[0, pl.ds(0, ROWS)], local_sem.at[0]),
        pltpu.make_async_copy(pos_in, cands.at[0, pl.ds(0, ROWS)], local_sem.at[1]),
        pltpu.make_async_copy(neg_in, cands.at[0, pl.ds(ROWS, NEGS)], local_sem.at[2]),
    ]
    for copy in locals_:
        copy.start()
    cmeta[0] = cmeta_in[...]
    qmeta[0, :, 0:ROWS] = qmeta_in[...]
    ymeta[0] = ymeta_in[...]

    peers = [along_z(s) for s in (1, 2, 3)]
    peers += [along_x(s, f) for s in range(4) for f in range(2) if (s, f) != (0, 0)]
    peers += [along_y(s) for s in (1, 2, 3)]
    barrier = pltpu.get_barrier_semaphore()
    for peer in peers:
        pl.semaphore_signal(barrier, inc=1, device_id=peer, device_id_type=MESH)
    pl.semaphore_wait(barrier, len(peers))

    qmeta_copies = {}
    for s in range(4):
        for f in range(2):
            if (s, f) != (0, 0):
                place = qmeta.at[PLACE[s], :, pl.ds(f * ROWS, ROWS)]
                qmeta_copies[(PLACE[s], f)] = remote(qmeta.at[0, :, pl.ds(0, ROWS)], place, along_x(s, f))
    cmeta_copies = {PLACE[s]: remote(cmeta.at[0], cmeta.at[PLACE[s]], along_z(s)) for s in (1, 2, 3)}
    ymeta_copies = [remote(ymeta.at[0], ymeta.at[s], along_y(s)) for s in (1, 2, 3)]
    for copy in (*qmeta_copies.values(), *cmeta_copies.values(), *ymeta_copies):
        go(copy)
    for copy in locals_:
        copy.wait()

    qh, ch = ROWS // 2, CANDS // 2

    def quer_at(p, half):
        return quers.at[p, pl.ds(half * qh, qh)]

    def cand_at(p, half):
        return cands.at[p, pl.ds(half * ch, ch)]

    sib = [
        remote(quers.at[p, pl.ds(0, ROWS)], quers.at[p, pl.ds(ROWS, ROWS)], along_x(0, 1)) for p in range(4)
    ]
    quer_up = [remote(quer_at(0, h), quer_at(1, h), along_x(1)) for h in (0, 1)]
    quer_down = [remote(quer_at(0, h), quer_at(2, h), along_x(-1)) for h in (0, 1)]
    quer_far = [
        remote(quer_at(1, 0), quer_at(3, 0), along_x(1)),
        remote(quer_at(2, 1), quer_at(3, 1), along_x(-1)),
    ]
    cand_up = [remote(cand_at(0, h), cand_at(1, h), along_z(1)) for h in (0, 1)]
    cand_down = [remote(cand_at(0, h), cand_at(2, h), along_z(-1)) for h in (0, 1)]
    cand_far = [
        remote(cand_at(1, 0), cand_at(3, 0), along_z(1)),
        remote(cand_at(2, 1), cand_at(3, 1), along_z(-1)),
    ]
    go(sib[0])
    go(quer_up[0])
    go(quer_down[1])
    go(cand_up[0])
    go(cand_down[1])
    go(quer_up[1])
    go(quer_down[0])
    go(cand_up[1])
    go(cand_down[0])

    stat[...] = jnp.concatenate(
        [jnp.full((4, 1, PAIR), FLOOR, F32), jnp.zeros((4, 1, PAIR), F32)], axis=0
    )

    def columns(p):
        for k in range(CANDS // 128):
            lanes = pl.ds(k * 128, 128)
            for row, ref in ((0, logq_col), (1, id_col)):
                ref[p, lanes, :] = jnp.broadcast_to(cmeta[p, row : row + 1, lanes], (128, 128)).T

    def on_target(r):
        r_index = lax.broadcasted_iota(jnp.int32, (CHUNK, PAIR), 0) + r * CHUNK
        q_index = lax.broadcasted_iota(jnp.int32, (CHUNK, PAIR), 1)
        return jnp.logical_and(r_index == q_index, q_index < ROWS)

    def tile(p, cs, diagonal):
        scores[p, cs] = lax.dot_general(
            cands[cs], quers[p], (((1,), (1,)), ((), ())), preferred_element_type=F32
        )
        row_ids = qmeta[p, 0:1, :]

        def mask(r, peak):
            rows = pl.ds(pl.multiple_of(r * CHUNK, CHUNK), CHUNK)
            s = scores[p, cs, rows, :] * (SCALE * LOG2E) - tiled(logq_col[cs, rows, :], PAIR // 128)
            drop = tiled(id_col[cs, rows, :], PAIR // 128) == row_ids
            if diagonal:
                drop = jnp.logical_and(drop, jnp.logical_not(on_target(r)))
            s = jnp.where(drop, FLOOR, s)
            scores[p, cs, rows, :] = s
            return jnp.maximum(peak, jnp.max(s.reshape(CHUNK // 8, 8, PAIR), axis=0))

        peak = lax.fori_loop(0, CANDS // CHUNK, mask, jnp.full((8, PAIR), FLOOR, F32), unroll=True)
        old = stat[p]
        new = jnp.maximum(old, jnp.max(peak, axis=0, keepdims=True))

        def add(r, total):
            rows = pl.ds(pl.multiple_of(r * CHUNK, CHUNK), CHUNK)
            e = jnp.exp2(scores[p, cs, rows, :] - new)
            return total + jnp.sum(e.reshape(CHUNK // 8, 8, PAIR), axis=0)

        total = lax.fori_loop(0, CANDS // CHUNK, add, jnp.zeros((8, PAIR), F32), unroll=True)
        stat[p] = new
        stat[4 + p] = stat[4 + p] * jnp.exp2(old - new) + jnp.sum(total, axis=0, keepdims=True)

    def tiles(p_first, p_count, c_first, c_count):
        @pl.loop(0, p_count * c_count)
        def _(t):
            tile(p_first + t % p_count, c_first + t // p_count, False)

    columns(0)
    sib[0].wait_recv()
    qmeta_copies[(0, 1)].wait_recv()
    tile(0, 0, True)
    quer_up[0].wait_recv()
    go(quer_far[0])
    quer_down[1].wait_recv()
    go(quer_far[1])
    cand_up[0].wait_recv()
    go(cand_far[0])
    cand_down[1].wait_recv()
    go(cand_far[1])
    quer_up[1].wait_recv()
    go(sib[1])
    quer_down[0].wait_recv()
    go(sib[2])
    sib[1].wait_recv()
    sib[2].wait_recv()
    for p in (1, 2):
        for f in (0, 1):
            qmeta_copies[(p, f)].wait_recv()
    tiles(1, 2, 0, 1)
    quer_far[0].wait_recv()
    quer_far[1].wait_recv()
    go(sib[3])
    cand_up[1].wait_recv()
    cand_down[0].wait_recv()
    for p in (1, 2):
        cmeta_copies[p].wait_recv()
        columns(p)
    tiles(0, 3, 1, 2)
    sib[3].wait_recv()
    for f in (0, 1):
        qmeta_copies[(3, f)].wait_recv()
    tiles(3, 1, 0, 3)
    cand_far[0].wait_recv()
    cand_far[1].wait_recv()
    cmeta_copies[3].wait_recv()
    columns(3)
    tiles(0, 4, 3, 1)

    def owner(p, f):
        core = (1 - c) if f else c
        return ((x + 4 - DIST[p]) % 4) * 2 + core

    for p in range(4):
        for f in range(2):
            row = pl.ds(owner(p, f), 1)
            lanes = slice(f * ROWS, (f + 1) * ROWS)
            stats[my_abs, 0, row, :] = stat[p][:, lanes]
            stats[my_abs, 1, row, :] = stat[4 + p][:, lanes]
    stat_copies = []
    for s in range(4):
        for f in range(2):
            if (s, f) != (0, 0):
                j = next(sems)
                go(remote(stats.at[my_abs], stats.at[my_abs], along_x(s, f), j))
                k = owner(PLACE[s], f)
                stat_copies.append(remote(stats.at[k], stats.at[k], along_x(s, f), j))
    for cs in range(4):
        cands_t[:, cs * CANDS : (cs + 1) * CANDS] = cands[cs].T
    for copy in stat_copies:
        copy.wait_recv()
    peak = stats[0, 0]
    for k in range(1, 8):
        peak = jnp.maximum(peak, stats[k, 0])
    total = jnp.zeros_like(peak)
    for k in range(8):
        total = total + stats[k, 1] * jnp.exp2(stats[k, 0] - peak)
    shift[...] = peak + jnp.log(total) * LOG2E
    lifts = []
    for p in range(4):
        lse = jnp.concatenate([shift[pl.ds(owner(p, f), 1), :] for f in range(2)], axis=1)
        lifts.append(jnp.log(qmeta[p, 1:2, :]) * LOG2E - lse)

    def cand_block(cs):
        @pl.loop(0, CANDS // CHUNK, unroll=4)
        def _(r):
            rows = pl.ds(pl.multiple_of(r * CHUNK, CHUNK), CHUNK)
            out = pl.ds(pl.multiple_of(cs * CANDS + r * CHUNK, CHUNK), CHUNK)
            for p in range(4):
                gw = jnp.exp2(scores[p, cs, rows, :] + lifts[p])
                if p == 0 and cs == 0:
                    gw = jnp.where(on_target(r), gw - qmeta[0, 1:2, :], gw)
                weights[out, p * PAIR : (p + 1) * PAIR] = gw.astype(BF16)

        cand_part[cs] = jnp.dot(
            weights[cs * CANDS : (cs + 1) * CANDS, :], quers[...].reshape(4 * PAIR, DIM),
            preferred_element_type=F32,
        )

    up, low = pl.ds(0, ch), pl.ds(ch, ch)
    relay_copies = [
        remote(cand_send.at[2, up], cand_relay.at[0], along_z(-1)),
        remote(cand_send.at[2, low], cand_relay.at[1], along_z(1)),
    ]
    to_down = [remote(cand_send.at[0, h], cand_got.at[0, h], along_z(-1)) for h in (up, low)]
    to_up = [remote(cand_send.at[1, h], cand_got.at[1, h], along_z(1)) for h in (up, low)]
    cand_block(3)
    cand_send[2] = cand_part[3].astype(BF16)
    go(relay_copies[1])
    go(relay_copies[0])
    cand_block(1)
    cand_send[0, low, :] = cand_part[1, low, :].astype(BF16)
    go(to_down[1])
    cand_block(2)
    cand_send[1, up, :] = cand_part[2, up, :].astype(BF16)
    go(to_up[0])
    relay_copies[1].wait_recv()
    cand_send[1, low, :] = (cand_part[2, low, :] + cand_relay[1].astype(F32)).astype(BF16)
    go(to_up[1])
    relay_copies[0].wait_recv()
    cand_send[0, up, :] = (cand_part[1, up, :] + cand_relay[0].astype(F32)).astype(BF16)
    go(to_down[0])
    cand_block(0)

    def quer_block(p):
        quer_part[p] = jnp.dot(
            cands_t[...], weights[:, p * PAIR : (p + 1) * PAIR], preferred_element_type=F32
        )
        sib_send[p] = quer_part[p, :, ROWS:PAIR].astype(BF16)
        go(sib_parts[p])

    def summed(p, rows):
        return quer_part[p, rows, 0:ROWS] + sib_got[p, rows, :].astype(F32)

    sib_parts = [remote(sib_send.at[p], sib_got.at[p], along_x(0, 1)) for p in range(4)]
    qup, qlow = pl.ds(0, DIM // 2), pl.ds(DIM // 2, DIM // 2)
    quer_relays = [
        remote(quer_send.at[2, qup], quer_relay.at[0], along_x(-1)),
        remote(quer_send.at[2, qlow], quer_relay.at[1], along_x(1)),
    ]
    q_down = [remote(quer_send.at[0, h], quer_got.at[0, h], along_x(-1)) for h in (qup, qlow)]
    q_up = [remote(quer_send.at[1, h], quer_got.at[1, h], along_x(1)) for h in (qup, qlow)]
    quer_block(3)
    quer_block(1)
    sib_parts[3].wait_recv()
    quer_send[2] = summed(3, slice(None)).astype(BF16)
    go(quer_relays[0])
    go(quer_relays[1])
    quer_block(2)
    sib_parts[1].wait_recv()
    quer_send[0, qlow, :] = summed(1, qlow).astype(BF16)
    go(q_down[1])
    quer_block(0)
    sib_parts[2].wait_recv()
    quer_send[1, qup, :] = summed(2, qup).astype(BF16)
    go(q_up[0])
    quer_relays[0].wait_recv()
    quer_send[0, qup, :] = (summed(1, qup) + quer_relay[0].astype(F32)).astype(BF16)
    go(q_down[0])
    quer_relays[1].wait_recv()
    quer_send[1, qlow, :] = (summed(2, qlow) + quer_relay[1].astype(F32)).astype(BF16)
    go(q_up[1])

    to_down[1].wait_recv()
    to_up[1].wait_recv()
    negs = pl.ds(ROWS, NEGS)
    neg_rows[0] = (
        cand_part[0, negs, :] + cand_got[0, negs, :].astype(F32) + cand_got[1, negs, :].astype(F32)
    )
    neg_copies = [remote(neg_rows.at[0], neg_rows.at[s], along_y(s)) for s in (1, 2, 3)]
    for copy in neg_copies:
        go(copy)
    to_down[0].wait_recv()
    to_up[0].wait_recv()
    item = pl.ds(0, ROWS)
    item_out[...] = (
        cand_part[0, item, :] + cand_got[0, item, :].astype(F32) + cand_got[1, item, :].astype(F32)
    )
    for copy in ymeta_copies:
        copy.wait_recv()
    for k in range(4):
        want = lax.broadcasted_iota(jnp.int32, (SLOTS, NEGS), 0) + g * SLOTS
        onehot[:, k * NEGS : (k + 1) * NEGS] = jnp.where(ymeta[k] == want, 1.0, 0.0).astype(BF16)

    sib_parts[0].wait_recv()
    for copy in (*q_down, *q_up):
        copy.wait_recv()
    qgt_out[...] = summed(0, slice(None)) + quer_got[0].astype(F32) + quer_got[1].astype(F32)

    for copy in neg_copies:
        copy.wait_recv()
    rows = neg_rows[...].reshape(4 * NEGS, DIM)
    high = rows.astype(BF16)
    rest = (rows - high.astype(F32)).astype(BF16)
    table_out[...] = jnp.dot(onehot[...], high, preferred_element_type=F32) + jnp.dot(
        onehot[...], rest, preferred_element_type=F32
    )
    for copy in sent:
        copy.wait_send()


def local(
    queries, pos_emb, pos_logq, pos_ids, row_weight, neg_emb, neg_logq, neg_ids, neg_owner, neg_slot
):
    cmeta = jnp.stack(
        [
            jnp.concatenate([pos_logq, neg_logq]).astype(F32) * LOG2E,
            jnp.concatenate([pos_ids, neg_ids]).astype(F32),
        ]
    )
    qmeta = jnp.stack([pos_ids.astype(F32), row_weight])
    ymeta = (neg_owner * SLOTS + neg_slot).reshape(1, NEGS)
    whole = pl.BlockSpec(memory_space=pltpu.VMEM)
    far = pl.BlockSpec(memory_space=pl.ANY)
    vmem = pltpu.VMEM
    query_grad_t, item_grad, table_grad = pl.pallas_call(
        kernel,
        out_shape=[
            jax.ShapeDtypeStruct((DIM, ROWS), F32),
            jax.ShapeDtypeStruct((ROWS, DIM), F32),
            jax.ShapeDtypeStruct((SLOTS, DIM), F32),
        ],
        in_specs=[far, far, far, whole, whole, whole],
        out_specs=[whole, whole, whole],
        scratch_shapes=[
            vmem((4, CANDS, DIM), BF16),
            vmem((DIM, 4 * CANDS), BF16),
            vmem((4, PAIR, DIM), BF16),
            vmem((4, 4, CANDS, PAIR), F32),
            vmem((4 * CANDS, 4 * PAIR), BF16),
            vmem((4, 2, CANDS), F32),
            vmem((4, 2, PAIR), F32),
            vmem((4, 1, NEGS), jnp.int32),
            vmem((4, CANDS, 128), F32),
            vmem((4, CANDS, 128), F32),
            vmem((8, 1, PAIR), F32),
            vmem((8, 2, 8, ROWS), F32),
            vmem((8, ROWS), F32),
            vmem((4, CANDS, DIM), F32),
            vmem((3, CANDS, DIM), BF16),
            vmem((2, CANDS // 2, DIM), BF16),
            vmem((2, CANDS, DIM), BF16),
            vmem((4, DIM, PAIR), F32),
            vmem((4, DIM, ROWS), BF16),
            vmem((4, DIM, ROWS), BF16),
            vmem((3, DIM, ROWS), BF16),
            vmem((2, DIM // 2, ROWS), BF16),
            vmem((2, DIM, ROWS), BF16),
            vmem((4, NEGS, DIM), F32),
            vmem((SLOTS, 4 * NEGS), BF16),
            pltpu.SemaphoreType.DMA((3,)),
            pltpu.SemaphoreType.DMA((64,)),
            pltpu.SemaphoreType.DMA((64,)),
        ],
        compiler_params=pltpu.CompilerParams(
            collective_id=0, has_side_effects=True, vmem_limit_bytes=60 * 2**20
        ),
        cost_estimate=pl.CostEstimate(flops=10 * 2**30, bytes_accessed=4 * 2**20, transcendentals=12 * 2**20),
    )(queries, pos_emb, neg_emb, cmeta, qmeta, ymeta)
    return query_grad_t.T * SCALE, item_grad * SCALE, table_grad * SCALE


def solution(mesh):
    rows = P(("group", "batch"), None)
    flat = P(("group", "batch"))
    in_specs = (rows, rows, flat, flat, flat, rows, flat, flat, flat, flat)
    return jax.shard_map(local, mesh=mesh, in_specs=in_specs, out_specs=(rows, rows, rows), check_vma=False)
```

time: 302 us -> 70.4 us (0.23)
  waiting for transfers between devices: 109 us -> 0 us
  matrix products: 80.6 us -> 0 us
  Pallas kernels: 0 us -> 60.1 us
  blocking collectives: 58.3 us -> 0 us
  other arithmetic: 18 us -> 4.34 us
  between operations: 14.1 us -> 0.68 us
  loops' own time: 6.32 us -> 0 us
  local copies, waits for them, and re-layouts: 10.2 us -> 4.89 us
  starting transfers between devices: 4.09 us -> 0 us
    reduce_scatter x1 -> x0, waiting for transfers between devices: 102 us -> none  [local(): lax.psum_scatter(jnp.dot(grad_cols, queries, preferred_element_type=jnp.f...]
    dot_general x18 -> x0, matrix products: 80.6 us -> none  [the longest x16 54.6 us: block_scores(): lax.dot_general(block_cands, queries, (((1,), (1,)), ((), ())), preferred...]
    pallas_call x0 -> x1, Pallas kernels: none -> 60.1 us  [local(): pl.pallas_call(kernel, out_shape=[jax.ShapeDtypeStruct((DIM, ROWS), F32),...]
    all_gather x2 -> x0, blocking collectives: 50.4 us -> none  [the longest x1 26.8 us: local(): lax.all_gather(local_logq, 'batch', axis=0, tiled=True)]
    reduce_sum x9 -> x0, other arithmetic: 10.4 us -> none  [the longest x8 10.2 us: stats_step(): jnp.sum(kept_terms, axis=0)]
    all_to_all x1 -> x0, blocking collectives: 7.9 us -> none  [local(): lax.all_to_all(send_slots, 'group', split_axis=0, concat_axis=0, tiled=True)]
    all_gather x1 -> x0, waiting for transfers between devices: 6.72 us -> none  [local(): lax.all_gather(local_cands, 'batch', axis=0, tiled=True)]
    another operation x2 -> x0, loops' own time: 6.32 us -> none  [the longest x1 5.51 us: local(): lax.map(make_block, jnp.arange(block_count, dtype=jnp.int32))]
  transfers between devices with their start and end apart: 3 -> 0, of which waited for: 2 -> 0; matrix products, arithmetic and copies ran while one was open for 5% -> 0% of each run, Pallas kernels for 0% -> 0%
where the time goes in v1:
time: 70.4 us; the launch traced here: 70 us
  Pallas kernels  60.1 us (85%)
  local copies, waits for them, and re-layouts  4.89 us (7%)
  other arithmetic  4.34 us (6%)
    pallas_call x1, Pallas kernels, local(): pl.pallas_call(kernel, out_shape=[jax.ShapeDtypeStruct((DIM, ROWS), F32),...  60.1 us
    unnamed x19, local copies, waits for them, and re-layouts  4.87 us
    mul x3, other arithmetic, local(): return (query_grad_t.T * SCALE, item_grad * SCALE, table_grad * SCALE)  2.62 us

profile of v1, /device:TPU:1, one launch (start us, length us, event | category | flops | bytes accessed | tf_op | source)
XLA Modules:
  0.0 70.0 jit_solution(9753717322186720522)
XLA Ops:
  0.6 0.0 copy-start.7
  0.6 0.0 copy-start.8
  0.7 0.6 copy-done.7
  1.3 0.0 copy-done.8
  1.3 0.0 copy-start.4
  1.3 0.5 add_bitcast_fusion.ymeta_in
  1.8 0.2 copy-done.4
  2.0 0.0 copy-start.5
  2.0 0.6 copy-done.5
  2.6 0.0 copy-start.3
  2.7 0.7 copy-done.3
  3.3 0.0 copy-start.2
  3.3 0.7 copy-done.2
  4.0 0.0 copy-start.6
  4.0 0.7 copy-done.6
  4.7 0.6 pad_maximum_fusion.cmeta_in
  5.3 0.6 pad_maximum_fusion.1.qmeta_in
  5.9 60.1 %shard_map.121 = (f32[256,384]{1,0:T(8,128)}, f32[384,256]{1,0:T(8,128)}, f32[512,256]{1,0:T(8,128)}) custom-call(bf16[384,256]{1,0:T(8,128)(2,1)} %q_in.1, bf16[384,256]{1,0:T(8,128)(2,1)} %pos_in.1, bf16[128,256]{1,0:T(8,128)(2,1)} %neg_in.1, f32[2,512]{1,0:T(2,128)} %pad_maximum_fusion.cmeta_in, f32[2,384]{1,0:T(2,128)} %pad_maximum_fusion.1.qmeta_in, ...), custom_call_target="tpu_custom_call" | custom-call | flops 10737418240 | bytes 4194304 | tf_op jit(solution)/shard_map/pallas_call | solution.py:393
  66.0 1.0 %multiply_bitcast_fusion = f32[384,256]{0,1:T(8,128)S(1)} fusion(f32[256,384]{1,0:T(8,128)} %get-tuple-element.6), kind=kLoop, calls=%fused_computation | loop fusion | flops 98304 | bytes 786432 | tf_op jit(solution)/shard_map/mul | solution.py:437
  67.0 0.0 copy-start.1
  67.0 0.9 %copy.13 = f32[384,256]{1,0:T(8,128)} copy(f32[384,256]{0,1:T(8,128)S(1)} %multiply_bitcast_fusion) | data formatting | bytes 786432
  67.9 0.1 copy-done.1
  68.0 0.0 copy-start
  68.0 0.8 %broadcast_multiply_fusion.1 = f32[384,256]{1,0:T(8,128)} fusion(f32[384,256]{1,0:T(8,128)S(1)} %copy-done.1), kind=kLoop, calls=%fused_computation.2 | loop fusion | flops 98304 | bytes 786432 | tf_op jit(solution)/shard_map/mul | solution.py:437
  68.8 0.4 copy-done
  69.2 0.8 %broadcast_multiply_fusion = f32[512,256]{1,0:T(8,128)} fusion(f32[512,256]{1,0:T(8,128)S(1)} %copy-done), kind=kLoop, calls=%fused_computation.1 | loop fusion | flops 131072 | bytes 1048576 | tf_op jit(solution)/shard_map/mul | solution.py:437
  (7 shorter events, 0.0 us)
Async XLA Ops:
  0.6 0.7 copy-start.7
  0.6 0.7 copy-start.8
  1.3 0.7 copy-start.4
  2.0 0.7 copy-start.5
  2.6 0.7 copy-start.3
  3.3 0.7 copy-start.2
  4.0 0.7 copy-start.6
  67.0 1.0 %copy-start.1 = (f32[384,256]{1,0:T(8,128)S(1)}, f32[384,256]{1,0:T(8,128)}, u32[]{:S(2)}) copy-start(f32[384,256]{1,0:T(8,128)} %get-tuple-element.7) | copy-start | bytes 1179652
  68.0 1.2 %copy-start = (f32[512,256]{1,0:T(8,128)S(1)}, f32[512,256]{1,0:T(8,128)}, u32[]{:S(2)}) copy-start(f32[512,256]{1,0:T(8,128)} %get-tuple-element.8) | copy-start | bytes 1572868

commit v2 on v1

v2 whole, which is shorter than its diff:
```python
import math

import jax
import jax.numpy as jnp
from jax import lax
from jax.experimental import pallas as pl
from jax.experimental.pallas import tpu as pltpu
from jax.sharding import PartitionSpec as P

MESH = pl.DeviceIdType.MESH
F32 = jnp.float32
BF16 = jnp.bfloat16
LOG2E = math.log2(math.e)
SCALE = 0.125
FLOOR = -1e30

ROWS = 384
NEGS = 128
CANDS = ROWS + NEGS
PAIR = 2 * ROWS
DIM = 256
SLOTS = 512
CHUNK = 32

DIST = (0, 1, 3, 2)
PLACE = (0, 1, 3, 2)


def tiled(x, count):
    return jnp.concatenate([x] * count, axis=1)


def kernel(
    q_in, pos_in, pos_logq_in, pos_ids_in, weight_in, neg_in, neg_logq_in, neg_ids_in, owner_in, slot_in,
    quer_out, item_out, table_out,
    cands, cands_t, quers, scores, raw_a, raw_b, terms, neg_weights, weights_a, weights_b,
    pos_logq, pos_ids, weight, neg_logq, neg_ids, neg_owner, neg_slot,
    cmeta, qmeta, ymeta, logq_col, id_col, stat, decay, stats, shift,
    neg_part, neg_send, neg_got, item_part, item_send, item_relay, item_got,
    quer_part, sib_send, sib_got, quer_send, quer_got,
    neg_rows, onehot, local_sem, send_sem, recv_sem,
):
    g = lax.axis_index("group")
    b = lax.axis_index("batch")
    z, x, c = b // 8, (b // 2) % 4, b % 2
    my_abs = x * 2 + c

    def along_z(step):
        return {"batch": ((z + step) % 4) * 8 + x * 2 + c}

    def along_x(step, flip=0):
        core = (1 - c) if flip else c
        return {"batch": z * 8 + ((x + step) % 4) * 2 + core}

    def along_y(step):
        return {"group": (g + step) % 4}

    sems = iter(range(80))
    sent = []

    def remote(src, dst, target, k=None):
        k = next(sems) if k is None else k
        return pltpu.make_async_remote_copy(
            src_ref=src, dst_ref=dst, send_sem=send_sem.at[k], recv_sem=recv_sem.at[k],
            device_id=target, device_id_type=MESH,
        )

    def go(copy):
        copy.start()
        sent.append(copy)

    peers = [along_z(s) for s in (1, 2, 3)]
    peers += [along_x(s, f) for s in range(4) for f in range(2) if (s, f) != (0, 0)]
    peers += [along_y(s) for s in (1, 2, 3)]
    barrier = pltpu.get_barrier_semaphore()
    for peer in peers:
        pl.semaphore_signal(barrier, inc=1, device_id=peer, device_id_type=MESH)

    pairs = [
        (q_in, quers.at[0, pl.ds(0, ROWS)]),
        (pos_in, cands.at[0, pl.ds(0, ROWS)]),
        (neg_in, cands.at[0, pl.ds(ROWS, NEGS)]),
        (pos_logq_in, pos_logq), (pos_ids_in, pos_ids), (weight_in, weight),
        (neg_logq_in, neg_logq), (neg_ids_in, neg_ids), (owner_in, neg_owner), (slot_in, neg_slot),
    ]
    locals_ = [pltpu.make_async_copy(src, dst, local_sem.at[k]) for k, (src, dst) in enumerate(pairs)]
    for copy in locals_:
        copy.start()
    for copy in locals_:
        copy.wait()
    cmeta[0, 0:1, 0:ROWS] = pos_logq[...].astype(F32).reshape(1, ROWS) * LOG2E
    cmeta[0, 0:1, ROWS:CANDS] = neg_logq[...].astype(F32).reshape(1, NEGS) * LOG2E
    cmeta[0, 1:2, 0:ROWS] = pos_ids[...].reshape(1, ROWS).astype(F32)
    cmeta[0, 1:2, ROWS:CANDS] = neg_ids[...].reshape(1, NEGS).astype(F32)
    qmeta[0, 0:1, 0:ROWS] = pos_ids[...].reshape(1, ROWS).astype(F32)
    qmeta[0, 1:2, 0:ROWS] = weight[...].reshape(1, ROWS)
    ymeta[0] = neg_owner[...].reshape(1, NEGS) * SLOTS + neg_slot[...].reshape(1, NEGS)

    def columns(p):
        cands_t[p] = cands[p].T
        for k in range(CANDS // 128):
            lanes = pl.ds(k * 128, 128)
            for row, ref in ((0, logq_col), (1, id_col)):
                ref[p, lanes, :] = jnp.broadcast_to(cmeta[p, row : row + 1, lanes], (128, 128)).T

    columns(0)
    stat[...] = jnp.concatenate(
        [jnp.full((4, 1, PAIR), FLOOR, F32), jnp.zeros((4, 1, PAIR), F32)], axis=0
    )
    quer_part[...] = jnp.zeros_like(quer_part)
    pl.semaphore_wait(barrier, len(peers))

    qh, ch = ROWS // 2, CANDS // 2

    def quer_at(p, half):
        return quers.at[p, pl.ds(half * qh, qh)]

    def cand_at(p, half):
        return cands.at[p, pl.ds(half * ch, ch)]

    sib = [
        remote(quers.at[p, pl.ds(0, ROWS)], quers.at[p, pl.ds(ROWS, ROWS)], along_x(0, 1)) for p in range(4)
    ]
    quer_up = [remote(quer_at(0, h), quer_at(1, h), along_x(1)) for h in (0, 1)]
    quer_down = [remote(quer_at(0, h), quer_at(2, h), along_x(-1)) for h in (0, 1)]
    quer_far = [
        remote(quer_at(1, 0), quer_at(3, 0), along_x(1)),
        remote(quer_at(2, 1), quer_at(3, 1), along_x(-1)),
    ]
    cand_up = [remote(cand_at(0, h), cand_at(1, h), along_z(1)) for h in (0, 1)]
    cand_down = [remote(cand_at(0, h), cand_at(2, h), along_z(-1)) for h in (0, 1)]
    cand_far = [
        remote(cand_at(1, 0), cand_at(3, 0), along_z(1)),
        remote(cand_at(2, 1), cand_at(3, 1), along_z(-1)),
    ]
    qmeta_copies = {}
    for s in range(4):
        for f in range(2):
            if (s, f) != (0, 0):
                place = qmeta.at[PLACE[s], :, pl.ds(f * ROWS, ROWS)]
                qmeta_copies[(PLACE[s], f)] = remote(qmeta.at[0, :, pl.ds(0, ROWS)], place, along_x(s, f))
    cmeta_copies = {PLACE[s]: remote(cmeta.at[0], cmeta.at[PLACE[s]], along_z(s)) for s in (1, 2, 3)}
    ymeta_copies = [remote(ymeta.at[0], ymeta.at[s], along_y(s)) for s in (1, 2, 3)]
    go(cand_up[0])
    go(cand_down[1])
    go(quer_up[0])
    go(quer_down[1])
    go(sib[0])
    go(qmeta_copies[(0, 1)])
    go(cand_up[1])
    go(cand_down[0])
    go(quer_up[1])
    go(quer_down[0])
    for key, copy in qmeta_copies.items():
        if key != (0, 1):
            go(copy)
    for copy in (*cmeta_copies.values(), *ymeta_copies):
        go(copy)

    def on_target(r):
        r_index = lax.broadcasted_iota(jnp.int32, (CHUNK, PAIR), 0) + r * CHUNK
        q_index = lax.broadcasted_iota(jnp.int32, (CHUNK, PAIR), 1)
        return jnp.logical_and(r_index == q_index, q_index < ROWS)

    def fold(p, cs):
        quer_part[p] = quer_part[p] * decay[...] + jnp.dot(
            cands_t[cs], terms[...], preferred_element_type=F32
        )

    def score(raw, p, cs):
        raw[...] = lax.dot_general(
            cands[cs], quers[p], (((1,), (1,)), ((), ())), preferred_element_type=F32
        )

    def expand(raw, p, cs, diagonal=False):
        row_ids = qmeta[p, 0:1, :]

        def mask(r, peak):
            rows = pl.ds(pl.multiple_of(r * CHUNK, CHUNK), CHUNK)
            s = raw[rows, :] * (SCALE * LOG2E) - tiled(logq_col[cs, rows, :], PAIR // 128)
            drop = tiled(id_col[cs, rows, :], PAIR // 128) == row_ids
            if diagonal:
                drop = jnp.logical_and(drop, jnp.logical_not(on_target(r)))
            s = jnp.where(drop, FLOOR, s)
            scores[p, cs, rows, :] = s
            return jnp.maximum(peak, jnp.max(s.reshape(CHUNK // 8, 8, PAIR), axis=0))

        peak = lax.fori_loop(0, CANDS // CHUNK, mask, jnp.full((8, PAIR), FLOOR, F32), unroll=True)
        old = stat[p]
        new = jnp.maximum(old, jnp.max(peak, axis=0, keepdims=True))

        def add(r, total):
            rows = pl.ds(pl.multiple_of(r * CHUNK, CHUNK), CHUNK)
            e = jnp.exp2(scores[p, cs, rows, :] - new)
            terms[rows, :] = e.astype(BF16)
            return total + jnp.sum(e.reshape(CHUNK // 8, 8, PAIR), axis=0)

        total = lax.fori_loop(0, CANDS // CHUNK, add, jnp.zeros((8, PAIR), F32), unroll=True)
        drop_to = jnp.exp2(old - new)
        decay[...] = drop_to
        stat[p] = new
        stat[4 + p] = stat[4 + p] * drop_to + jnp.sum(total, axis=0, keepdims=True)

    def block(t):
        p = jnp.where(t < 3, t, jnp.where(t < 9, t % 3, jnp.where(t < 12, 3, t - 12)))
        cs = jnp.where(t < 3, 0, jnp.where(t < 9, t // 3, jnp.where(t < 12, t - 9, 3)))
        return p, cs

    def arrived(t, at, do):
        @pl.when(t == at)
        def _():
            do()

    def candidates_from(p, copies):
        def do():
            for copy in (*copies, cmeta_copies[p]):
                copy.wait_recv()
            columns(p)
            if p == 2:
                quer_far[0].wait_recv()
                quer_far[1].wait_recv()
                sib[3].start()

        return do

    def queries_from(p):
        def do():
            sib[p].wait_recv()
            for f in (0, 1):
                qmeta_copies[(p, f)].wait_recv()

        return do

    sib[0].wait_recv()
    qmeta_copies[(0, 1)].wait_recv()
    score(raw_a, 0, 0)
    expand(raw_a, 0, 0, True)
    quer_up[0].wait_recv()
    go(quer_far[0])
    quer_down[1].wait_recv()
    go(quer_far[1])
    cand_up[0].wait_recv()
    go(cand_far[0])
    cand_down[1].wait_recv()
    go(cand_far[1])
    quer_up[1].wait_recv()
    go(sib[1])
    quer_down[0].wait_recv()
    go(sib[2])
    queries_from(1)()
    score(raw_b, 1, 0)

    @pl.loop(0, 7)
    def _(i):
        t = 2 * i + 1
        arrived(t, 1, queries_from(2))
        arrived(t, 5, candidates_from(2, (cand_down[0],)))
        arrived(t, 11, candidates_from(3, cand_far))
        score(raw_a, *block(t + 1))
        fold(*block(t - 1))
        expand(raw_b, *block(t))
        arrived(t, 1, candidates_from(1, (cand_up[1],)))
        arrived(t, 7, queries_from(3))
        score(raw_b, *block(t + 2))
        fold(*block(t))
        expand(raw_a, *block(t + 1))

    sent.append(sib[3])
    fold(*block(14))
    expand(raw_b, *block(15))

    def owner(p, f):
        core = (1 - c) if f else c
        return ((x + 4 - DIST[p]) % 4) * 2 + core

    for p in range(4):
        part = stat[p] + jnp.log(stat[4 + p]) * LOG2E
        for f in range(2):
            stats[my_abs, pl.ds(owner(p, f), 1), :] = part[:, f * ROWS : (f + 1) * ROWS]
    stat_copies = []
    for s in (2, 1, 3, 0):
        for f in range(2):
            if (s, f) != (0, 0):
                j = next(sems)
                go(remote(stats.at[my_abs], stats.at[my_abs], along_x(s, f), j))
                k = owner(PLACE[s], f)
                stat_copies.append(remote(stats.at[k], stats.at[k], along_x(s, f), j))
    fold(*block(15))
    for copy in ymeta_copies:
        copy.wait_recv()
    for k in range(4):
        want = lax.broadcasted_iota(jnp.int32, (SLOTS, NEGS), 0) + g * SLOTS
        onehot[:, k * NEGS : (k + 1) * NEGS] = jnp.where(ymeta[k] == want, 1.0, 0.0).astype(BF16)
    for copy in stat_copies:
        copy.wait_recv()
    peak = stats[0]
    for k in range(1, 8):
        peak = jnp.maximum(peak, stats[k])
    total = jnp.zeros_like(peak)
    for k in range(8):
        total = total + jnp.exp2(stats[k] - peak)
    shift[...] = peak + jnp.log(total) * LOG2E
    lifts, factors = [], []
    for p in range(4):
        lse = jnp.concatenate([shift[pl.ds(owner(p, f), 1), :] for f in range(2)], axis=1)
        lifts.append(jnp.log(qmeta[p, 1:2, :]) * LOG2E - lse)
        factors.append(qmeta[p, 1:2, :] * jnp.exp2(stat[p] - lse))

    sib_parts = [remote(sib_send.at[p], sib_got.at[p], along_x(0, 1)) for p in range(4)]
    for p in (3, 1, 2, 0):
        sib_send[p] = (quer_part[p, :, ROWS:PAIR] * factors[p][:, ROWS:PAIR]).astype(BF16)
        go(sib_parts[p])

    def weigh(cs, r, out, place):
        rows = pl.ds(pl.multiple_of(r * CHUNK, CHUNK), CHUNK)
        for p in range(4):
            gw = jnp.exp2(scores[p, cs, rows, :] + lifts[p])
            if p == 0 and cs == 0:
                gw = jnp.where(on_target(r), gw - qmeta[0, 1:2, :], gw)
            out[place, p * PAIR : (p + 1) * PAIR] = gw.astype(BF16)

    all_quers = quers[...].reshape(4 * PAIR, DIM)

    def weigh_items(cs, out):
        def do(r, carry):
            weigh(cs, r, out, pl.ds(pl.multiple_of(r * CHUNK, CHUNK), CHUNK))
            return carry

        lax.fori_loop(0, ROWS // CHUNK, do, 0, unroll=True)

    for cs in range(4):
        for r in range(NEGS // CHUNK):
            weigh(cs, ROWS // CHUNK + r, neg_weights, pl.ds(cs * NEGS + r * CHUNK, CHUNK))
    neg_part[...] = jnp.dot(neg_weights[...], all_quers, preferred_element_type=F32).reshape(4, NEGS, DIM)
    weigh_items(3, weights_a)
    neg_copies = []
    for p, step in ((3, 2), (1, -1), (2, 1)):
        neg_send[p - 1] = neg_part[p].astype(BF16)
        copy = remote(neg_send.at[p - 1], neg_got.at[p - 1], along_z(step))
        go(copy)
        neg_copies.append(copy)

    def item_block(cs, held, after=None, out=None):
        item_part[cs] = jnp.dot(held[...], all_quers, preferred_element_type=F32)
        if out is not None:
            weigh_items(after, out)

    def summed(p):
        return quer_part[p, :, 0:ROWS] * factors[p][:, 0:ROWS] + sib_got[p].astype(F32)

    quer_copies = []
    for p, step in ((3, 2), (1, -1), (2, 1)):
        sib_parts[p].wait_recv()
        quer_send[p - 1] = summed(p).astype(BF16)
        copy = remote(quer_send.at[p - 1], quer_got.at[p - 1], along_x(step))
        go(copy)
        quer_copies.append(copy)

    ih = ROWS // 2
    up, low = pl.ds(0, ih), pl.ds(ih, ih)
    relay_copies = [
        remote(item_send.at[2, up], item_relay.at[0], along_z(-1)),
        remote(item_send.at[2, low], item_relay.at[1], along_z(1)),
    ]
    to_down = [remote(item_send.at[0, h], item_got.at[0, h], along_z(-1)) for h in (up, low)]
    to_up = [remote(item_send.at[1, h], item_got.at[1, h], along_z(1)) for h in (up, low)]
    item_block(3, weights_a, 1, weights_b)
    item_send[2] = item_part[3].astype(BF16)
    go(relay_copies[1])
    go(relay_copies[0])
    item_block(1, weights_b, 2, weights_a)
    item_send[0, low, :] = item_part[1, low, :].astype(BF16)
    go(to_down[1])
    item_block(2, weights_a, 0, weights_b)
    item_send[1, up, :] = item_part[2, up, :].astype(BF16)
    go(to_up[0])
    item_block(0, weights_b)
    for copy in neg_copies:
        copy.wait_recv()
    neg_rows[0] = (
        neg_part[0] + neg_got[0].astype(F32) + neg_got[1].astype(F32) + neg_got[2].astype(F32)
    ).astype(BF16)
    y_copies = [remote(neg_rows.at[0], neg_rows.at[s], along_y(s)) for s in (2, 1, 3)]
    for copy in y_copies:
        go(copy)
    relay_copies[1].wait_recv()
    item_send[1, low, :] = (item_part[2, low, :] + item_relay[1].astype(F32)).astype(BF16)
    go(to_up[1])
    relay_copies[0].wait_recv()
    item_send[0, up, :] = (item_part[1, up, :] + item_relay[0].astype(F32)).astype(BF16)
    go(to_down[0])

    sib_parts[0].wait_recv()
    own = summed(0) - cands_t[0, :, 0:ROWS].astype(F32) * qmeta[0, 1:2, 0:ROWS]
    for copy in quer_copies:
        copy.wait_recv()
    own = own + quer_got[0].astype(F32) + quer_got[1].astype(F32) + quer_got[2].astype(F32)
    quer_out[...] = (own * SCALE).T
    for copy in y_copies:
        copy.wait_recv()
    table_out[...] = SCALE * jnp.dot(
        onehot[...], neg_rows[...].reshape(4 * NEGS, DIM), preferred_element_type=F32
    )
    for copy in (*to_down, *to_up):
        copy.wait_recv()
    item_out[...] = SCALE * (item_part[0] + item_got[0].astype(F32) + item_got[1].astype(F32))
    for copy in sent:
        copy.wait_send()


def copy_kernel(*refs):
    sems = refs[-1]
    copies = [pltpu.make_async_copy(refs[k], refs[3 + k], sems.at[k]) for k in range(3)]
    for copy in copies:
        copy.start()
    for copy in copies:
        copy.wait()


def local(*args):
    far = pl.BlockSpec(memory_space=pl.ANY)
    here = pl.BlockSpec(memory_space=pltpu.VMEM)
    vmem = pltpu.VMEM
    out_shape = [
        jax.ShapeDtypeStruct((ROWS, DIM), F32),
        jax.ShapeDtypeStruct((ROWS, DIM), F32),
        jax.ShapeDtypeStruct((SLOTS, DIM), F32),
    ]
    results = pl.pallas_call(
        kernel,
        out_shape=[pltpu.VMEM(o.shape, o.dtype) for o in out_shape],
        in_specs=[far] * 10,
        out_specs=[here] * 3,
        scratch_shapes=[
            vmem((4, CANDS, DIM), BF16),
            vmem((4, DIM, CANDS), BF16),
            vmem((4, PAIR, DIM), BF16),
            vmem((4, 4, CANDS, PAIR), F32),
            vmem((CANDS, PAIR), F32),
            vmem((CANDS, PAIR), F32),
            vmem((CANDS, PAIR), BF16),
            vmem((4 * NEGS, 4 * PAIR), BF16),
            vmem((ROWS, 4 * PAIR), BF16),
            vmem((ROWS, 4 * PAIR), BF16),
            vmem((ROWS,), BF16), vmem((ROWS,), jnp.int32), vmem((ROWS,), F32),
            vmem((NEGS,), BF16), vmem((NEGS,), jnp.int32), vmem((NEGS,), jnp.int32), vmem((NEGS,), jnp.int32),
            vmem((4, 2, CANDS), F32),
            vmem((4, 2, PAIR), F32),
            vmem((4, 1, NEGS), jnp.int32),
            vmem((4, CANDS, 128), F32),
            vmem((4, CANDS, 128), F32),
            vmem((8, 1, PAIR), F32),
            vmem((1, PAIR), F32),
            vmem((8, 8, ROWS), F32),
            vmem((8, ROWS), F32),
            vmem((4, NEGS, DIM), F32),
            vmem((3, NEGS, DIM), BF16),
            vmem((3, NEGS, DIM), BF16),
            vmem((4, ROWS, DIM), F32),
            vmem((3, ROWS, DIM), BF16),
            vmem((2, ROWS // 2, DIM), BF16),
            vmem((2, ROWS, DIM), BF16),
            vmem((4, DIM, PAIR), F32),
            vmem((4, DIM, ROWS), BF16),
            vmem((4, DIM, ROWS), BF16),
            vmem((3, DIM, ROWS), BF16),
            vmem((3, DIM, ROWS), BF16),
            vmem((4, NEGS, DIM), BF16),
            vmem((SLOTS, 4 * NEGS), BF16),
            pltpu.SemaphoreType.DMA((10,)),
            pltpu.SemaphoreType.DMA((80,)),
            pltpu.SemaphoreType.DMA((80,)),
        ],
        compiler_params=pltpu.CompilerParams(
            collective_id=0, has_side_effects=True, vmem_limit_bytes=54 * 2**20
        ),
        cost_estimate=pl.CostEstimate(flops=10 * 2**30, bytes_accessed=4 * 2**20, transcendentals=12 * 2**20),
    )(*args)
    return pl.pallas_call(
        copy_kernel,
        out_shape=out_shape,
        in_specs=[here] * 3,
        out_specs=[far] * 3,
        scratch_shapes=[pltpu.SemaphoreType.DMA((3,))],
        compiler_params=pltpu.CompilerParams(vmem_limit_bytes=2**20),
    )(*results)


def solution(mesh):
    rows = P(("group", "batch"), None)
    flat = P(("group", "batch"))
    in_specs = (rows, rows, flat, flat, flat, rows, flat, flat, flat, flat)
    return jax.shard_map(local, mesh=mesh, in_specs=in_specs, out_specs=(rows, rows, rows), check_vma=False)
```

time: 70.4 us -> 49.5 us (0.70)
  Pallas kernels: 60.1 us -> 48.8 us
  local copies, waits for them, and re-layouts: 4.89 us -> 0 us
  other arithmetic: 4.34 us -> 0 us
    pallas_call x1 -> x2, Pallas kernels: 60.1 us -> 48.8 us  [the longest x1 47.7 us: local(): pl.pallas_call(kernel, out_shape=[pltpu.VMEM(o.shape, o.dtype) for o in o...]
    unnamed x19 -> x0, local copies, waits for them, and re-layouts: 4.87 us -> none
    mul x4 -> x0, other arithmetic: 2.63 us -> none  [the longest x3 2.62 us: local(): return (query_grad_t.T * SCALE, item_grad * SCALE, table_grad * SCALE)]
    another operation x2 -> x0, other arithmetic: 1.19 us -> none  [the longest x1 0.6 us: local(): jnp.stack([jnp.concatenate([pos_logq, neg_logq]).astype(F32) * LOG2E, jnp...]
where the time goes in v2:
time: 49.5 us; the launch traced here: 49.4 us
  Pallas kernels  48.8 us (99%)
  between operations  0.64 us (1%)
    pallas_call x1, Pallas kernels, local(): pl.pallas_call(kernel, out_shape=[pltpu.VMEM(o.shape, o.dtype) for o in o...  47.7 us
    pallas_call x1, Pallas kernels, local(): pl.pallas_call(copy_kernel, out_shape=out_shape, in_specs=[here] * 3, out...  1.08 us

profile of v2, /device:TPU:1, one launch (start us, length us, event | category | flops | bytes accessed | tf_op | source)
XLA Modules:
  0.0 49.4 jit_solution(6200720438615800011)
XLA Ops:
  0.6 47.7 %shard_map.121 = (f32[384,256]{1,0:T(8,128)S(1)}, f32[384,256]{1,0:T(8,128)S(1)}, f32[512,256]{1,0:T(8,128)S(1)}) custom-call(bf16[384,256]{1,0:T(8,128)(2,1)} %q_in.1, bf16[384,256]{1,0:T(8,128)(2,1)} %pos_in.1, bf16[384]{0:T(512)(128)(2,1)} %pos_logq_in.1, s32[384]{0:T(512)} %pos_ids_in.1, f32[384]{0:T(512)} %weight_in.1, bf16[128,256]{1,0:T(8,128)(2,1)} %neg_in.1, ...), custom_call_target="tpu_custom_call" | custom-call | flops 10737418240 | bytes 4194304 | tf_op jit(solution)/shard_map/pallas_call | solution.py:429
  48.3 1.1 %shard_map.122 = (f32[384,256]{1,0:T(8,128)}, f32[384,256]{1,0:T(8,128)}, f32[512,256]{1,0:T(8,128)}) custom-call(f32[384,256]{1,0:T(8,128)S(1)} %get-tuple-element.6.refs_0_, f32[384,256]{1,0:T(8,128)S(1)} %get-tuple-element.7.refs_1_, f32[512,256]{1,0:T(8,128)S(1)} %get-tuple-element.8.refs_2_), custom_call_target="tpu_custom_call" | custom-call | tf_op jit(solution)/shard_map/pallas_call | solution.py:479

commit v3 on v2

--- a/solution.py
+++ b/solution.py
@@ -21,6 +21,8 @@
 DIM = 256
 SLOTS = 512
 CHUNK = 32
+TALL = DIM + 16
+WIDE = PAIR
 
 DIST = (0, 1, 3, 2)
 PLACE = (0, 1, 3, 2)
@@ -86,7 +88,39 @@
     locals_ = [pltpu.make_async_copy(src, dst, local_sem.at[k]) for k, (src, dst) in enumerate(pairs)]
     for copy in locals_:
         copy.start()
-    for copy in locals_:
+    for copy in locals_[:3]:
+        copy.wait()
+    pl.semaphore_wait(barrier, len(peers))
+    qh, ch = ROWS // 2, CANDS // 2
+
+    def quer_at(p, half):
+        return quers.at[p, pl.ds(half * qh, qh)]
+
+    def cand_at(p, half):
+        return cands.at[p, pl.ds(half * ch, ch)]
+
+    sib = [
+        remote(quers.at[p, pl.ds(0, ROWS)], quers.at[p, pl.ds(ROWS, ROWS)], along_x(0, 1)) for p in range(4)
+    ]
+    own_quers = quers.at[0, pl.ds(0, ROWS)]
+    quer_up = remote(own_quers, quers.at[1, pl.ds(0, ROWS)], along_x(1))
+    quer_down = remote(own_quers, quers.at[2, pl.ds(0, ROWS)], along_x(-1))
+    quer_far = [
+        remote(quer_at(1, 0), quer_at(3, 0), along_x(1)),
+        remote(quer_at(2, 1), quer_at(3, 1), along_x(-1)),
+    ]
+    cand_up = remote(cands.at[0], cands.at[1], along_z(1))
+    cand_down = remote(cands.at[0], cands.at[2], along_z(-1))
+    cand_far = [
+        remote(cand_at(1, 0), cand_at(3, 0), along_z(1)),
+        remote(cand_at(2, 1), cand_at(3, 1), along_z(-1)),
+    ]
+    go(cand_up)
+    go(cand_down)
+    go(quer_up)
+    go(quer_down)
+    go(sib[0])
+    for copy in locals_[3:]:
         copy.wait()
     cmeta[0, 0:1, 0:ROWS] = pos_logq[...].astype(F32).reshape(1, ROWS) * LOG2E
     cmeta[0, 0:1, ROWS:CANDS] = neg_logq[...].astype(F32).reshape(1, NEGS) * LOG2E
@@ -97,42 +131,13 @@
     ymeta[0] = neg_owner[...].reshape(1, NEGS) * SLOTS + neg_slot[...].reshape(1, NEGS)
 
     def columns(p):
-        cands_t[p] = cands[p].T
+        cands_t[p, 0:DIM, :] = cands[p].T
         for k in range(CANDS // 128):
             lanes = pl.ds(k * 128, 128)
             for row, ref in ((0, logq_col), (1, id_col)):
                 ref[p, lanes, :] = jnp.broadcast_to(cmeta[p, row : row + 1, lanes], (128, 128)).T
 
-    columns(0)
-    stat[...] = jnp.concatenate(
-        [jnp.full((4, 1, PAIR), FLOOR, F32), jnp.zeros((4, 1, PAIR), F32)], axis=0
-    )
-    quer_part[...] = jnp.zeros_like(quer_part)
-    pl.semaphore_wait(barrier, len(peers))
-
-    qh, ch = ROWS // 2, CANDS // 2
-
-    def quer_at(p, half):
-        return quers.at[p, pl.ds(half * qh, qh)]
-
-    def cand_at(p, half):
-        return cands.at[p, pl.ds(half * ch, ch)]
-
-    sib = [
-        remote(quers.at[p, pl.ds(0, ROWS)], quers.at[p, pl.ds(ROWS, ROWS)], along_x(0, 1)) for p in range(4)
-    ]
-    quer_up = [remote(quer_at(0, h), quer_at(1, h), along_x(1)) for h in (0, 1)]
-    quer_down = [remote(quer_at(0, h), quer_at(2, h), along_x(-1)) for h in (0, 1)]
-    quer_far = [
-        remote(quer_at(1, 0), quer_at(3, 0), along_x(1)),
-        remote(quer_at(2, 1), quer_at(3, 1), along_x(-1)),
-    ]
-    cand_up = [remote(cand_at(0, h), cand_at(1, h), along_z(1)) for h in (0, 1)]
-    cand_down = [remote(cand_at(0, h), cand_at(2, h), along_z(-1)) for h in (0, 1)]
-    cand_far = [
-        remote(cand_at(1, 0), cand_at(3, 0), along_z(1)),
-        remote(cand_at(2, 1), cand_at(3, 1), along_z(-1)),
-    ]
+
     qmeta_copies = {}
     for s in range(4):
         for f in range(2):
@@ -141,158 +146,168 @@
                 qmeta_copies[(PLACE[s], f)] = remote(qmeta.at[0, :, pl.ds(0, ROWS)], place, along_x(s, f))
     cmeta_copies = {PLACE[s]: remote(cmeta.at[0], cmeta.at[PLACE[s]], along_z(s)) for s in (1, 2, 3)}
     ymeta_copies = [remote(ymeta.at[0], ymeta.at[s], along_y(s)) for s in (1, 2, 3)]
-    go(cand_up[0])
-    go(cand_down[1])
-    go(quer_up[0])
-    go(quer_down[1])
-    go(sib[0])
     go(qmeta_copies[(0, 1)])
-    go(cand_up[1])
-    go(cand_down[0])
-    go(quer_up[1])
-    go(quer_down[0])
     for key, copy in qmeta_copies.items():
         if key != (0, 1):
             go(copy)
     for copy in (*cmeta_copies.values(), *ymeta_copies):
         go(copy)
 
-    def on_target(r):
-        r_index = lax.broadcasted_iota(jnp.int32, (CHUNK, PAIR), 0) + r * CHUNK
-        q_index = lax.broadcasted_iota(jnp.int32, (CHUNK, PAIR), 1)
+    columns(0)
+    stat[...] = jnp.full((4, 1, PAIR), FLOOR, F32)
+    cands_t[:, DIM:TALL, :] = jnp.ones((4, TALL - DIM, CANDS), BF16)
+    quer_part[...] = jnp.zeros_like(quer_part)
+
+    def on_target(r, first=0, width=PAIR):
+        r_index = lax.broadcasted_iota(jnp.int32, (CHUNK, width), 0) + r * CHUNK
+        q_index = lax.broadcasted_iota(jnp.int32, (CHUNK, width), 1) + first
         return jnp.logical_and(r_index == q_index, q_index < ROWS)
 
-    def fold(p, cs):
-        quer_part[p] = quer_part[p] * decay[...] + jnp.dot(
-            cands_t[cs], terms[...], preferred_element_type=F32
+    def score(raw, p, cs, n):
+        raw[:, n : n + WIDE] = lax.dot_general(
+            cands[cs], quers[p, n : n + WIDE, :], (((1,), (1,)), ((), ())), preferred_element_type=F32
         )
 
-    def score(raw, p, cs):
-        raw[...] = lax.dot_general(
-            cands[cs], quers[p], (((1,), (1,)), ((), ())), preferred_element_type=F32
+    def fold(p, cs, n):
+        quer_part[p, :, n : n + WIDE] = quer_part[p, :, n : n + WIDE] * decay[:, n : n + WIDE] + jnp.dot(
+            cands_t[cs], terms[:, n : n + WIDE], preferred_element_type=F32
         )
 
-    def expand(raw, p, cs, diagonal=False):
-        row_ids = qmeta[p, 0:1, :]
+    def expand(raw, p, cs, n, diagonal=False):
+        lanes = slice(n, n + WIDE)
+        row_ids = qmeta[p, 0:1, lanes]
 
         def mask(r, peak):
             rows = pl.ds(pl.multiple_of(r * CHUNK, CHUNK), CHUNK)
-            s = raw[rows, :] * (SCALE * LOG2E) - tiled(logq_col[cs, rows, :], PAIR // 128)
-            drop = tiled(id_col[cs, rows, :], PAIR // 128) == row_ids
+            s = raw[rows, lanes] * (SCALE * LOG2E) - tiled(logq_col[cs, rows, :], WIDE // 128)
+            drop = tiled(id_col[cs, rows, :], WIDE // 128) == row_ids
             if diagonal:
-                drop = jnp.logical_and(drop, jnp.logical_not(on_target(r)))
+                drop = jnp.logical_and(drop, jnp.logical_not(on_target(r, n, WIDE)))
             s = jnp.where(drop, FLOOR, s)
-            scores[p, cs, rows, :] = s
-            return jnp.maximum(peak, jnp.max(s.reshape(CHUNK // 8, 8, PAIR), axis=0))
-
-        peak = lax.fori_loop(0, CANDS // CHUNK, mask, jnp.full((8, PAIR), FLOOR, F32), unroll=True)
-        old = stat[p]
+            scores[p, cs, rows, lanes] = s
+            return jnp.maximum(peak, jnp.max(s.reshape(CHUNK // 8, 8, WIDE), axis=0))
+
+        peak = lax.fori_loop(0, CANDS // CHUNK, mask, jnp.full((8, WIDE), FLOOR, F32), unroll=True)
+        old = stat[p, :, lanes]
         new = jnp.maximum(old, jnp.max(peak, axis=0, keepdims=True))
 
-        def add(r, total):
+        def add(r, carry):
             rows = pl.ds(pl.multiple_of(r * CHUNK, CHUNK), CHUNK)
-            e = jnp.exp2(scores[p, cs, rows, :] - new)
-            terms[rows, :] = e.astype(BF16)
-            return total + jnp.sum(e.reshape(CHUNK // 8, 8, PAIR), axis=0)
-
-        total = lax.fori_loop(0, CANDS // CHUNK, add, jnp.zeros((8, PAIR), F32), unroll=True)
-        drop_to = jnp.exp2(old - new)
-        decay[...] = drop_to
-        stat[p] = new
-        stat[4 + p] = stat[4 + p] * drop_to + jnp.sum(total, axis=0, keepdims=True)
-
-    def block(t):
-        p = jnp.where(t < 3, t, jnp.where(t < 9, t % 3, jnp.where(t < 12, 3, t - 12)))
-        cs = jnp.where(t < 3, 0, jnp.where(t < 9, t // 3, jnp.where(t < 12, t - 9, 3)))
-        return p, cs
-
-    def arrived(t, at, do):
-        @pl.when(t == at)
-        def _():
-            do()
+            terms[rows, lanes] = jnp.exp2(scores[p, cs, rows, lanes] - new).astype(BF16)
+            return carry
+
+        lax.fori_loop(0, CANDS // CHUNK, add, 0, unroll=True)
+        decay[:, lanes] = jnp.exp2(old - new)
+        stat[p, :, lanes] = new
+
+    def step(now, raw, ahead=None, raw_ahead=None, before=None, diagonal=False):
+        for n in range(0, PAIR, WIDE):
+            if ahead is not None:
+                score(raw_ahead, *ahead, n)
+            if before is not None:
+                fold(*before, n)
+            expand(raw, *now, n, diagonal)
+
+    order = [(p, 0) for p in range(3)] + [(p, cs) for cs in (1, 2) for p in range(3)]
+    order += [(3, cs) for cs in range(3)] + [(p, 3) for p in range(4)]
 
     def candidates_from(p, copies):
-        def do():
-            for copy in (*copies, cmeta_copies[p]):
-                copy.wait_recv()
-            columns(p)
-            if p == 2:
-                quer_far[0].wait_recv()
-                quer_far[1].wait_recv()
-                sib[3].start()
-
-        return do
+        for copy in (*copies, cmeta_copies[p]):
+            copy.wait_recv()
+        columns(p)
 
     def queries_from(p):
-        def do():
-            sib[p].wait_recv()
-            for f in (0, 1):
-                qmeta_copies[(p, f)].wait_recv()
-
-        return do
+        sib[p].wait_recv()
+        for f in (0, 1):
+            qmeta_copies[(p, f)].wait_recv()
 
     sib[0].wait_recv()
     qmeta_copies[(0, 1)].wait_recv()
-    score(raw_a, 0, 0)
-    expand(raw_a, 0, 0, True)
-    quer_up[0].wait_recv()
+    for n in range(0, PAIR, WIDE):
+        score(raw_a, 0, 0, n)
+    step((0, 0), raw_a, diagonal=True)
+    quer_up.wait_recv()
+    go(sib[1])
+    quer_down.wait_recv()
+    go(sib[2])
     go(quer_far[0])
-    quer_down[1].wait_recv()
     go(quer_far[1])
-    cand_up[0].wait_recv()
+    cand_up.wait_recv()
     go(cand_far[0])
-    cand_down[1].wait_recv()
+    cand_down.wait_recv()
     go(cand_far[1])
-    quer_up[1].wait_recv()
-    go(sib[1])
-    quer_down[0].wait_recv()
-    go(sib[2])
-    queries_from(1)()
-    score(raw_b, 1, 0)
-
-    @pl.loop(0, 7)
-    def _(i):
-        t = 2 * i + 1
-        arrived(t, 1, queries_from(2))
-        arrived(t, 5, candidates_from(2, (cand_down[0],)))
-        arrived(t, 11, candidates_from(3, cand_far))
-        score(raw_a, *block(t + 1))
-        fold(*block(t - 1))
-        expand(raw_b, *block(t))
-        arrived(t, 1, candidates_from(1, (cand_up[1],)))
-        arrived(t, 7, queries_from(3))
-        score(raw_b, *block(t + 2))
-        fold(*block(t))
-        expand(raw_a, *block(t + 1))
-
-    sent.append(sib[3])
-    fold(*block(14))
-    expand(raw_b, *block(15))
+    queries_from(1)
+    score(raw_b, 1, 0, 0)
+    raws = (raw_a, raw_b)
+    for t in range(1, 16):
+        ahead = order[t + 1] if t < 15 else None
+        if ahead == (2, 0):
+            queries_from(2)
+        elif ahead == (0, 1):
+            candidates_from(1, ())
+        elif ahead == (0, 2):
+            candidates_from(2, ())
+            quer_far[0].wait_recv()
+            quer_far[1].wait_recv()
+            go(sib[3])
+        elif ahead == (3, 0):
+            queries_from(3)
+        elif ahead == (0, 3):
+            candidates_from(3, cand_far)
+        step(order[t], raws[t % 2], ahead, raws[(t + 1) % 2], order[t - 1])
+    fold(*order[15], 0)
 
     def owner(p, f):
         core = (1 - c) if f else c
         return ((x + 4 - DIST[p]) % 4) * 2 + core
 
+    def count(p):
+        return quer_part[p, DIM : DIM + 1, :]
+
     for p in range(4):
-        part = stat[p] + jnp.log(stat[4 + p]) * LOG2E
+        part = stat[p] + jnp.log(count(p)) * LOG2E
         for f in range(2):
             stats[my_abs, pl.ds(owner(p, f), 1), :] = part[:, f * ROWS : (f + 1) * ROWS]
-    stat_copies = []
+    stat_copies = {}
     for s in (2, 1, 3, 0):
         for f in range(2):
             if (s, f) != (0, 0):
                 j = next(sems)
                 go(remote(stats.at[my_abs], stats.at[my_abs], along_x(s, f), j))
                 k = owner(PLACE[s], f)
-                stat_copies.append(remote(stats.at[k], stats.at[k], along_x(s, f), j))
-    fold(*block(15))
+                stat_copies[(s, f)] = remote(stats.at[k], stats.at[k], along_x(s, f), j)
+
+    sib_parts = [remote(sib_send.at[p], sib_got.at[p], along_x(0, 1)) for p in range(4)]
+    for p in (3, 1, 2, 0):
+        share = 1.0 / count(p)[:, ROWS:PAIR]
+        sib_send[p] = (quer_part[p, 0:DIM, ROWS:PAIR] * share).astype(BF16)
+        go(sib_parts[p])
+    stat_copies[(0, 1)].wait_recv()
+
+    def chip_average(p):
+        row = pl.ds(owner(p, 0), 1)
+        mine, other = stats[my_abs, row, :], stats[owner(0, 1), row, :]
+        top = jnp.maximum(mine, other)
+        mine, other = jnp.exp2(mine - top), jnp.exp2(other - top)
+        both = 1.0 / (mine + other)
+        mine, other = mine * both / count(p)[:, 0:ROWS], other * both
+        return quer_part[p, 0:DIM, 0:ROWS] * mine + sib_got[p].astype(F32) * other
+
+    quer_copies = []
+    for p, step_x in ((3, 2), (1, -1), (2, 1)):
+        sib_parts[p].wait_recv()
+        quer_send[p - 1] = chip_average(p).astype(BF16)
+        copy = remote(quer_send.at[p - 1], quer_got.at[p - 1], along_x(step_x))
+        go(copy)
+        quer_copies.append(copy)
     for copy in ymeta_copies:
         copy.wait_recv()
     for k in range(4):
         want = lax.broadcasted_iota(jnp.int32, (SLOTS, NEGS), 0) + g * SLOTS
         onehot[:, k * NEGS : (k + 1) * NEGS] = jnp.where(ymeta[k] == want, 1.0, 0.0).astype(BF16)
-    for copy in stat_copies:
-        copy.wait_recv()
+    for key, copy in stat_copies.items():
+        if key != (0, 1):
+            copy.wait_recv()
     peak = stats[0]
     for k in range(1, 8):
         peak = jnp.maximum(peak, stats[k])
@@ -300,16 +315,10 @@
     for k in range(8):
         total = total + jnp.exp2(stats[k] - peak)
     shift[...] = peak + jnp.log(total) * LOG2E
-    lifts, factors = [], []
+    lifts = []
     for p in range(4):
         lse = jnp.concatenate([shift[pl.ds(owner(p, f), 1), :] for f in range(2)], axis=1)
         lifts.append(jnp.log(qmeta[p, 1:2, :]) * LOG2E - lse)
-        factors.append(qmeta[p, 1:2, :] * jnp.exp2(stat[p] - lse))
-
-    sib_parts = [remote(sib_send.at[p], sib_got.at[p], along_x(0, 1)) for p in range(4)]
-    for p in (3, 1, 2, 0):
-        sib_send[p] = (quer_part[p, :, ROWS:PAIR] * factors[p][:, ROWS:PAIR]).astype(BF16)
-        go(sib_parts[p])
 
     def weigh(cs, r, out, place):
         rows = pl.ds(pl.multiple_of(r * CHUNK, CHUNK), CHUNK)
@@ -344,17 +353,6 @@
         item_part[cs] = jnp.dot(held[...], all_quers, preferred_element_type=F32)
         if out is not None:
             weigh_items(after, out)
-
-    def summed(p):
-        return quer_part[p, :, 0:ROWS] * factors[p][:, 0:ROWS] + sib_got[p].astype(F32)
-
-    quer_copies = []
-    for p, step in ((3, 2), (1, -1), (2, 1)):
-        sib_parts[p].wait_recv()
-        quer_send[p - 1] = summed(p).astype(BF16)
-        copy = remote(quer_send.at[p - 1], quer_got.at[p - 1], along_x(step))
-        go(copy)
-        quer_copies.append(copy)
 
     ih = ROWS // 2
     up, low = pl.ds(0, ih), pl.ds(ih, ih)
@@ -390,11 +388,18 @@
     item_send[0, up, :] = (item_part[1, up, :] + item_relay[0].astype(F32)).astype(BF16)
     go(to_down[0])
 
+    my_row = pl.ds(my_abs, 1)
+
+    def chip_weight(step):
+        k = ((x + step) % 4) * 2
+        return sum(jnp.exp2(stats[k + f, my_row, :] - shift[my_row, :]) for f in range(2))
+
     sib_parts[0].wait_recv()
-    own = summed(0) - cands_t[0, :, 0:ROWS].astype(F32) * qmeta[0, 1:2, 0:ROWS]
-    for copy in quer_copies:
-        copy.wait_recv()
-    own = own + quer_got[0].astype(F32) + quer_got[1].astype(F32) + quer_got[2].astype(F32)
+    own = chip_average(0) * chip_weight(0)
+    for k, step_x in ((2, 2), (0, 1), (1, 3)):
+        quer_copies[(1, 2, 0)[k]].wait_recv()
+        own = own + quer_got[k].astype(F32) * chip_weight(step_x)
+    own = (own - cands_t[0, 0:DIM, 0:ROWS].astype(F32)) * qmeta[0, 1:2, 0:ROWS]
     quer_out[...] = (own * SCALE).T
     for copy in y_copies:
         copy.wait_recv()
@@ -433,7 +438,7 @@
         out_specs=[here] * 3,
         scratch_shapes=[
             vmem((4, CANDS, DIM), BF16),
-            vmem((4, DIM, CANDS), BF16),
+            vmem((4, TALL, CANDS), BF16),
             vmem((4, PAIR, DIM), BF16),
             vmem((4, 4, CANDS, PAIR), F32),
             vmem((CANDS, PAIR), F32),
@@ -449,7 +454,7 @@
             vmem((4, 1, NEGS), jnp.int32),
             vmem((4, CANDS, 128), F32),
             vmem((4, CANDS, 128), F32),
-            vmem((8, 1, PAIR), F32),
+            vmem((4, 1, PAIR), F32),
             vmem((1, PAIR), F32),
             vmem((8, 8, ROWS), F32),
             vmem((8, ROWS), F32),
@@ -460,7 +465,7 @@
             vmem((3, ROWS, DIM), BF16),
             vmem((2, ROWS // 2, DIM), BF16),
             vmem((2, ROWS, DIM), BF16),
-            vmem((4, DIM, PAIR), F32),
+            vmem((4, TALL, PAIR), F32),
             vmem((4, DIM, ROWS), BF16),
             vmem((4, DIM, ROWS), BF16),
             vmem((3, DIM, ROWS), BF16),

time: 49.5 us -> 48.2 us (0.974)
  Pallas kernels: 48.8 us -> 47.2 us
    pallas_call x1, Pallas kernels: 47.7 us -> 46.1 us  [local(): pl.pallas_call(kernel, out_shape=[pltpu.VMEM(o.shape, o.dtype) for o in o...]
where the time goes in v3:
time: 48.2 us; the launch traced here: 48 us
  Pallas kernels  47.2 us (98%)
  between operations  0.8 us (2%)
    pallas_call x1, Pallas kernels, local(): pl.pallas_call(kernel, out_shape=[pltpu.VMEM(o.shape, o.dtype) for o in o...  46.1 us
    pallas_call x1, Pallas kernels, local(): pl.pallas_call(copy_kernel, out_shape=out_shape, in_specs=[here] * 3, out...  1.08 us

profile of v3, /device:TPU:1, one launch (start us, length us, event | category | flops | bytes accessed | tf_op | source)
XLA Modules:
  0.0 48.0 jit_solution(2430123302441125302)
XLA Ops:
  0.6 46.1 %shard_map.121 = (f32[384,256]{1,0:T(8,128)S(1)}, f32[384,256]{1,0:T(8,128)S(1)}, f32[512,256]{1,0:T(8,128)S(1)}) custom-call(bf16[384,256]{1,0:T(8,128)(2,1)} %q_in.1, bf16[384,256]{1,0:T(8,128)(2,1)} %pos_in.1, bf16[384]{0:T(512)(128)(2,1)} %pos_logq_in.1, s32[384]{0:T(512)} %pos_ids_in.1, f32[384]{0:T(512)} %weight_in.1, bf16[128,256]{1,0:T(8,128)(2,1)} %neg_in.1, ...), custom_call_target="tpu_custom_call" | custom-call | flops 10737418240 | bytes 4194304 | tf_op jit(solution)/shard_map/pallas_call | solution.py:434
  46.8 1.1 %shard_map.122 = (f32[384,256]{1,0:T(8,128)}, f32[384,256]{1,0:T(8,128)}, f32[512,256]{1,0:T(8,128)}) custom-call(f32[384,256]{1,0:T(8,128)S(1)} %get-tuple-element.6.refs_0_, f32[384,256]{1,0:T(8,128)S(1)} %get-tuple-element.7.refs_1_, f32[512,256]{1,0:T(8,128)S(1)} %get-tuple-element.8.refs_2_), custom_call_target="tpu_custom_call" | custom-call | tf_op jit(solution)/shard_map/pallas_call | solution.py:484

commit v4 on v3

--- a/solution.py
+++ b/solution.py
@@ -337,17 +337,23 @@
 
         lax.fori_loop(0, ROWS // CHUNK, do, 0, unroll=True)
 
-    for cs in range(4):
-        for r in range(NEGS // CHUNK):
-            weigh(cs, ROWS // CHUNK + r, neg_weights, pl.ds(cs * NEGS + r * CHUNK, CHUNK))
-    neg_part[...] = jnp.dot(neg_weights[...], all_quers, preferred_element_type=F32).reshape(4, NEGS, DIM)
+    neg_copies = []
+    steps_z = {3: 2, 1: -1, 2: 1}
+    for group in ((2, 3), (0, 1)):
+        for cs in group:
+            for r in range(NEGS // CHUNK):
+                weigh(cs, ROWS // CHUNK + r, neg_weights, pl.ds(cs * NEGS + r * CHUNK, CHUNK))
+        first, count_rows = min(group), len(group) * NEGS
+        neg_part[first : first + len(group)] = jnp.dot(
+            neg_weights[first * NEGS : first * NEGS + count_rows, :], all_quers, preferred_element_type=F32
+        ).reshape(len(group), NEGS, DIM)
+        for cs in group:
+            if cs:
+                neg_send[cs - 1] = neg_part[cs].astype(BF16)
+                copy = remote(neg_send.at[cs - 1], neg_got.at[cs - 1], along_z(steps_z[cs]))
+                go(copy)
+                neg_copies.append(copy)
     weigh_items(3, weights_a)
-    neg_copies = []
-    for p, step in ((3, 2), (1, -1), (2, 1)):
-        neg_send[p - 1] = neg_part[p].astype(BF16)
-        copy = remote(neg_send.at[p - 1], neg_got.at[p - 1], along_z(step))
-        go(copy)
-        neg_copies.append(copy)
 
     def item_block(cs, held, after=None, out=None):
         item_part[cs] = jnp.dot(held[...], all_quers, preferred_element_type=F32)

time: 48.2 us -> 46.7 us (0.969)
  Pallas kernels: 47.2 us -> 45.4 us
    pallas_call x1, Pallas kernels: 46.1 us -> 44.3 us  [local(): pl.pallas_call(kernel, out_shape=[pltpu.VMEM(o.shape, o.dtype) for o in o...]
where the time goes in v4:
time: 46.7 us; the launch traced here: 46.2 us
  Pallas kernels  45.4 us (97%)
  between operations  0.8 us (2%)
    pallas_call x1, Pallas kernels, local(): pl.pallas_call(kernel, out_shape=[pltpu.VMEM(o.shape, o.dtype) for o in o...  44.3 us
    pallas_call x1, Pallas kernels, local(): pl.pallas_call(copy_kernel, out_shape=out_shape, in_specs=[here] * 3, out...  1.08 us

profile of v4, /device:TPU:1, one launch (start us, length us, event | category | flops | bytes accessed | tf_op | source)
XLA Modules:
  0.0 46.2 jit_solution(6919828773422649086)
XLA Ops:
  0.6 44.3 %shard_map.121 = (f32[384,256]{1,0:T(8,128)S(1)}, f32[384,256]{1,0:T(8,128)S(1)}, f32[512,256]{1,0:T(8,128)S(1)}) custom-call(bf16[384,256]{1,0:T(8,128)(2,1)} %q_in.1, bf16[384,256]{1,0:T(8,128)(2,1)} %pos_in.1, bf16[384]{0:T(512)(128)(2,1)} %pos_logq_in.1, s32[384]{0:T(512)} %pos_ids_in.1, f32[384]{0:T(512)} %weight_in.1, bf16[128,256]{1,0:T(8,128)(2,1)} %neg_in.1, ...), custom_call_target="tpu_custom_call" | custom-call | flops 10737418240 | bytes 4194304 | tf_op jit(solution)/shard_map/pallas_call | solution.py:440
  45.0 1.1 %shard_map.122 = (f32[384,256]{1,0:T(8,128)}, f32[384,256]{1,0:T(8,128)}, f32[512,256]{1,0:T(8,128)}) custom-call(f32[384,256]{1,0:T(8,128)S(1)} %get-tuple-element.6.refs_0_, f32[384,256]{1,0:T(8,128)S(1)} %get-tuple-element.7.refs_1_, f32[512,256]{1,0:T(8,128)S(1)} %get-tuple-element.8.refs_2_), custom_call_target="tpu_custom_call" | custom-call | tf_op jit(solution)/shard_map/pallas_call | solution.py:490

commit v5 on v4

--- a/solution.py
+++ b/solution.py
@@ -347,13 +347,14 @@
         neg_part[first : first + len(group)] = jnp.dot(
             neg_weights[first * NEGS : first * NEGS + count_rows, :], all_quers, preferred_element_type=F32
         ).reshape(len(group), NEGS, DIM)
+        if 0 in group:
+            weigh_items(3, weights_a)
         for cs in group:
             if cs:
                 neg_send[cs - 1] = neg_part[cs].astype(BF16)
                 copy = remote(neg_send.at[cs - 1], neg_got.at[cs - 1], along_z(steps_z[cs]))
                 go(copy)
                 neg_copies.append(copy)
-    weigh_items(3, weights_a)
 
     def item_block(cs, held, after=None, out=None):
         item_part[cs] = jnp.dot(held[...], all_quers, preferred_element_type=F32)

time: 46.7 us -> 46.7 us (level)
  no operation moved by 1% of the time
where the time goes in v5:
time: 46.7 us; the launch traced here: 46.2 us
  Pallas kernels  45.4 us (97%)
  between operations  0.8 us (2%)
    pallas_call x1, Pallas kernels, local(): pl.pallas_call(kernel, out_shape=[pltpu.VMEM(o.shape, o.dtype) for o in o...  44.3 us
    pallas_call x1, Pallas kernels, local(): pl.pallas_call(copy_kernel, out_shape=out_shape, in_specs=[here] * 3, out...  1.08 us

profile of v5, /device:TPU:1, one launch (start us, length us, event | category | flops | bytes accessed | tf_op | source)
XLA Modules:
  0.0 46.2 jit_solution(6919828773422649086)
XLA Ops:
  0.6 44.3 %shard_map.121 = (f32[384,256]{1,0:T(8,128)S(1)}, f32[384,256]{1,0:T(8,128)S(1)}, f32[512,256]{1,0:T(8,128)S(1)}) custom-call(bf16[384,256]{1,0:T(8,128)(2,1)} %q_in.1, bf16[384,256]{1,0:T(8,128)(2,1)} %pos_in.1, bf16[384]{0:T(512)(128)(2,1)} %pos_logq_in.1, s32[384]{0:T(512)} %pos_ids_in.1, f32[384]{0:T(512)} %weight_in.1, bf16[128,256]{1,0:T(8,128)(2,1)} %neg_in.1, ...), custom_call_target="tpu_custom_call" | custom-call | flops 10737418240 | bytes 4194304 | tf_op jit(solution)/shard_map/pallas_call | solution.py:441
  45.0 1.1 %shard_map.122 = (f32[384,256]{1,0:T(8,128)}, f32[384,256]{1,0:T(8,128)}, f32[512,256]{1,0:T(8,128)}) custom-call(f32[384,256]{1,0:T(8,128)S(1)} %get-tuple-element.6.refs_0_, f32[384,256]{1,0:T(8,128)S(1)} %get-tuple-element.7.refs_1_, f32[512,256]{1,0:T(8,128)S(1)} %get-tuple-element.8.refs_2_), custom_call_target="tpu_custom_call" | custom-call | tf_op jit(solution)/shard_map/pallas_call | solution.py:491
